TPU v7x, 128 devices: a whole 4x4x4 slice. The times are simulated.
128 devices in a mesh: expert: 64 (over y, x, z), head: 2 (over core).
Axes of the slice: x: 4, y: 4, z: 4, core: 2. Of those that a mesh axis runs over, the one named last changes fastest.
Arguments:
- tokens: bfloat16 [8192, 4096], P('expert'), may hold values from -6 to 6
- router_weight: bfloat16 [4096, 64], replicated, may hold values from -16 to 16
- gate_weight: bfloat16 [64, 4096, 1536], P('expert', None, 'head'), may hold values from -0.09375 to 0.09375
- up_weight: bfloat16 [64, 4096, 1536], P('expert', None, 'head'), may hold values from -0.09375 to 0.09375
- down_weight: bfloat16 [64, 1536, 4096], P('expert', 'head'), may hold values from -0.15625 to 0.15625
- head_weight: bfloat16 [4096], replicated, may hold values from -0.09375 to 0.09375
- expert_ids: int32 [8192, 8], P('expert'), may hold values from 0 to 63, all different within a row; in each aligned block of 128 rows (0 to 127, 128 to 255, ...) at most 18 rows name the same one
- lengths: int32 [64, 4], replicated, may hold values from 1 to 48, 128 in all within a row
- pairs: int32 [128, 2], replicated, may hold values from 0 to 255, as said below
Outputs:
- token_grad: bfloat16 [8192, 4096], P('expert', 'head')
Inputs may be any that keep to these rules, and one draw needn't show every extreme that they name: `expert_ids`: each row names 8 different experts; among the rows of one group no expert is named more than 18 times. `lengths`: each row sums to 128. `pairs`: every sequence number appears exactly once.
All inputs are finite; a program needn't handle non-finite values.
Results may differ from a plain program's by a relative error of at most 0.02.
Values may be sent and summed in bfloat16 or wider, within the bound.
No kernel may reach another device: no remote copies, remote signals or barrier semaphores. Data moves between devices by JAX's collectives and lax.ppermute only.
A program may use at most 128 MiB of HBM per device.

v0:
```python
import functools

import jax
import jax.numpy as jnp
from jax import lax
from jax.experimental import pallas as pl
from jax.experimental.pallas import tpu as pltpu
from jax.sharding import PartitionSpec as P

LOSS_SCALE = 1024
MAIN = 8
LANES = 128
SWAP = [(0, 1), (1, 0)]
F32 = jnp.float32
BF16 = jnp.bfloat16


def split_three(x):
    high = lax.reduce_precision(x, 8, 7)
    middle = lax.reduce_precision(x - high, 8, 7)
    low = x - high - middle
    return high.astype(BF16), middle.astype(BF16), low.astype(BF16)


def exchange(x):
    return lax.all_to_all(x, "expert", split_axis=0, concat_axis=0, tiled=True)


def swap(x):
    return lax.ppermute(x, "head", SWAP)


def pick(rows, cols, first, axis):
    a = lax.broadcasted_iota(jnp.int32, (rows, cols), axis)
    b = lax.broadcasted_iota(jnp.int32, (rows, cols), 1 - axis)
    return (b == a * MAIN + first).astype(BF16)


def shuffle(rows, groups):
    a = lax.broadcasted_iota(jnp.int32, (rows, rows), 0)
    b = lax.broadcasted_iota(jnp.int32, (rows, rows), 1)
    return (b == (a % groups) * MAIN + a // groups).astype(BF16)


def slot_order():
    return [*range(MAIN), 2 * MAIN, *range(MAIN, 2 * MAIN), 2 * MAIN + 1]


def pieces_of(x):
    high = x.astype(BF16)
    rest = x - high.astype(F32)
    middle = rest.astype(BF16)
    return high, middle, (rest - middle.astype(F32)).astype(BF16)


def spread_pieces(x, cap):
    line = jnp.zeros(x.shape, F32)
    for i, piece in enumerate(pieces_of(x)):
        piece = piece.astype(F32)
        line = line + (pltpu.roll(piece, i * cap, 1) if i else piece)
    return line.astype(BF16)


def join_pieces(line, cap):
    return (
        line + pltpu.roll(line, LANES - cap, 1) + pltpu.roll(line, LANES - 2 * cap, 1)
    )


def touch_kernel(*refs):
    pass


def touch(x, *after):
    return pl.pallas_call(
        touch_kernel,
        out_shape=jax.ShapeDtypeStruct(x.shape, x.dtype),
        in_specs=[pl.BlockSpec(memory_space=pl.ANY)] * (1 + len(after)),
        out_specs=pl.BlockSpec(memory_space=pl.ANY),
        input_output_aliases={0: 0},
    )(x, *after)


def forward_kernel(
    span,
    steps,
    cap,
    head_ref,
    own_hbm,
    other_hbm,
    wg_ref,
    wu_ref,
    hm_ref,
    before_ref,
    after_ref,
    dg_ref,
    du_ref,
    score_ref,
    own_ref,
    other_ref,
    x_ref,
    gate_ref,
    up_ref,
    column_ref,
    stack_ref,
    in_sems,
):
    step = pl.program_id(0)
    main_rows, lanes = own_ref.shape
    groups = main_rows // MAIN
    rows = gate_ref.shape[0]
    halves = steps // 2
    half = halves * span
    piece = half // MAIN
    pieces = span // piece
    own_cols = [slice(i * span, (i + 1) * span) for i in range(halves)] + [slice(half, lanes)]

    def own_in(i):
        cols = own_cols[i]
        return pltpu.make_async_copy(own_hbm.at[:, cols], own_ref.at[:, cols], in_sems.at[i])

    def other_in():
        return pltpu.make_async_copy(other_hbm.at[:, :lanes], other_ref, in_sems.at[halves + 1])

    def gather_extra(src):
        stack_ref[...] = jnp.dot(
            shuffle(main_rows, groups), src[:, half : half + piece], preferred_element_type=F32
        ).astype(BF16)

    def fill(src, chunk):
        x_ref[:main_rows, :] = src[:, chunk * span : (chunk + 1) * span]
        for j in range(pieces):
            q = chunk * pieces + j
            x_ref[main_rows:, j * piece : (j + 1) * piece] = stack_ref[
                q * groups : (q + 1) * groups, :
            ]

    for i in range(steps):

        @pl.when(step == i)
        def _(i=i):
            if i == 0:
                for number in (0, halves, *range(1, halves)):
                    own_in(number).start()
                other_in().start()
                own_in(halves).wait()
                gather_extra(own_ref)
            if i < halves:
                own_in(i).wait()
                fill(own_ref, i)
            else:
                if i == halves:
                    other_in().wait()
                    gather_extra(other_ref)
                fill(other_ref, i - halves)

    @pl.when(step == 0)
    def _():
        gate_ref[...] = jnp.dot(x_ref[...], wg_ref[...], preferred_element_type=F32)
        up_ref[...] = jnp.dot(x_ref[...], wu_ref[...], preferred_element_type=F32)

    @pl.when(step > 0)
    def _():
        gate_ref[...] += jnp.dot(x_ref[...], wg_ref[...], preferred_element_type=F32)
        up_ref[...] += jnp.dot(x_ref[...], wu_ref[...], preferred_element_type=F32)

    @pl.when(step == steps - 1)
    def _():
        block = 64
        head_map = hm_ref[...]

        def body(i, carry):
            here = pl.ds(pl.multiple_of(i * block, block), block)
            gate = gate_ref[here, :]
            up = up_ref[here, :]
            sig = 1.0 / (1.0 + jnp.exp(-gate))
            act = gate * sig
            hidden = (act * up).astype(BF16).astype(F32)
            column_ref[here, :] = jnp.sum(hidden * head_map, axis=1, keepdims=True)
            du_ref[here, :] = (head_map * act).astype(BF16)
            dg_ref[here, :] = (head_map * up * sig * (1.0 + gate * (1.0 - sig))).astype(BF16)
            return carry

        lax.fori_loop(0, rows // block, body, 0)
        place = lax.broadcasted_iota(jnp.int32, (main_rows, LANES), 0) % MAIN
        lane = lax.broadcasted_iota(jnp.int32, (main_rows, LANES), 1)
        table = jnp.where(lane == place, column_ref[:main_rows, :], 0.0)
        a = lax.broadcasted_iota(jnp.int32, (groups, main_rows), 0)
        b = lax.broadcasted_iota(jnp.int32, (groups, main_rows), 1)
        fold = ((b >= a * MAIN) & (b < a * MAIN + MAIN)).astype(BF16)
        folded = sum(jnp.dot(fold, t, preferred_element_type=F32) for t in pieces_of(table))
        lane = lax.broadcasted_iota(jnp.int32, (groups, LANES), 1)
        score = jnp.where(lane == MAIN, column_ref[main_rows:, :], folded)
        if cap is None:
            score_ref[...] = score
        else:
            score = jnp.where(lane <= MAIN, before_ref[...], pltpu.roll(score, MAIN + 1, 1))
            score = jnp.where(lane < cap, score, 0.0)
            score_ref[...] = score
            du_ref[rows:, :] = jnp.zeros((groups, du_ref.shape[1]), BF16)
            du_ref[rows:, :LANES] = spread_pieces(score, cap)


def forward_call(cap, head, own, other, w_gate, w_up, head_map, before, after):
    main_rows = own.shape[0]
    width, hidden = w_gate.shape
    groups = main_rows // MAIN
    half = width // 2
    lanes = half + half // MAIN
    span = 1024
    steps = width // span
    rows = main_rows + groups
    out_rows = rows if cap is None else rows + groups

    def weight_at(i, head_ref):
        return (lax.rem(head_ref[0] * (steps // 2) + i, steps), 0)

    fixed = lambda i, head_ref: (0, 0)
    anywhere = pl.BlockSpec(memory_space=pl.ANY)
    return pl.pallas_call(
        functools.partial(forward_kernel, span, steps, cap),
        grid_spec=pltpu.PrefetchScalarGridSpec(
            num_scalar_prefetch=1,
            grid=(steps,),
            in_specs=[
                anywhere,
                anywhere,
                pl.BlockSpec((span, hidden), weight_at),
                pl.BlockSpec((span, hidden), weight_at),
                pl.BlockSpec((1, hidden), fixed),
                pl.BlockSpec(before.shape, fixed),
                anywhere,
            ],
            out_specs=[
                pl.BlockSpec((rows, hidden), fixed),
                pl.BlockSpec((out_rows, hidden), fixed),
                pl.BlockSpec((groups, LANES), fixed),
            ],
            scratch_shapes=[
                pltpu.VMEM((main_rows, lanes), BF16),
                pltpu.VMEM((main_rows, lanes), BF16),
                pltpu.VMEM((rows, span), BF16),
                pltpu.VMEM((rows, hidden), F32),
                pltpu.VMEM((rows, hidden), F32),
                pltpu.VMEM((rows, 1), F32),
                pltpu.VMEM((main_rows, half // MAIN), BF16),
                pltpu.SemaphoreType.DMA((steps // 2 + 2,)),
            ],
        ),
        out_shape=[
            jax.ShapeDtypeStruct((rows, hidden), BF16),
            jax.ShapeDtypeStruct((out_rows, hidden), BF16),
            jax.ShapeDtypeStruct((groups, LANES), F32),
        ],
        compiler_params=pltpu.CompilerParams(
            dimension_semantics=("arbitrary",), vmem_limit_bytes=62 << 20
        ),
    )(head, own, other, w_gate, w_up, head_map, before, after)


def make_side(cap, own, other, side_in, base, rows):
    groups = own.shape[0]
    seqs = base.shape[1]
    lines = seqs // LANES
    seq_dev = seqs // groups
    lane = lax.broadcasted_iota(jnp.int32, (groups, LANES), 1)
    scores = jnp.where(lane < cap, own + join_pieces(other, cap), 0.0)
    seq_in = pltpu.roll(side_in, LANES - 3 * cap, 1)
    weighted = jnp.where(lane < cap, join_pieces(side_in, cap) * scores, 0.0)
    a = lax.broadcasted_iota(jnp.int32, (groups, seqs), 0)
    b = lax.broadcasted_iota(jnp.int32, (groups, seqs), 1)
    table = jnp.zeros((groups, seqs), F32)
    for j in range(seq_dev):
        part = jnp.sum(jnp.where(seq_in == float(j), weighted, 0.0), axis=1, keepdims=True)
        table = jnp.where(b == a * seq_dev + j, part, table)
    reward = jnp.sum(table, axis=0, keepdims=True) + base
    place = lax.broadcasted_iota(jnp.int32, (rows, LANES), 0) % MAIN
    side = jnp.zeros((rows, LANES), F32)
    for i, piece in enumerate(pieces_of(reward)):
        for line in range(lines):
            values = piece[:, line * LANES : (line + 1) * LANES].astype(F32)
            side = jnp.where(place == i * lines + line, values, side)
    chosen = pick(rows, groups, 3 * lines, 1)
    side = side + jnp.dot(chosen, spread_pieces(scores, cap), preferred_element_type=F32)
    return side.astype(BF16)


def backward_kernel(span, steps, cap, head_ref, *refs):
    if cap is None:
        dg0, du0, dg1, du1, wg0, wu0, wg1, wu1, out_hbm, out_ref, stack_ref, sems = refs
    else:
        (dg0, du0, dg1, du1, wg0, wu0, wg1, wu1, own_ref, base_ref, recv_hbm) = refs[:11]
        out_hbm, out_ref, stack_ref, sems, given_ref = refs[11:]
    step = pl.program_id(0)
    main_rows, lanes = out_ref.shape
    groups = main_rows // MAIN
    rows = dg0.shape[0]
    half = steps * span
    piece = half // MAIN
    pieces = span // piece

    def given():
        return pltpu.make_async_copy(
            recv_hbm.at[:, half + piece :], given_ref, sems.at[steps + 1]
        )

    def leaving(i):
        cols = slice(i * span, (i + 1) * span) if i < steps else slice(half, lanes)
        return pltpu.make_async_copy(out_ref.at[:, cols], out_hbm.at[:, cols], sems.at[i])

    for chunk in range(steps):

        @pl.when(step == chunk)
        def _(chunk=chunk):
            if chunk == 0 and cap is not None:
                given().start()
            dims = (((1,), (1,)), ((), ()))
            value = 0.0
            for grad, weight in ((dg0, wg0), (du0, wu0), (dg1, wg1), (du1, wu1)):
                value = value + lax.dot_general(
                    grad[:rows, :], weight[...], dims, preferred_element_type=F32
                )
            value = value.astype(BF16)
            out_ref[:, chunk * span : (chunk + 1) * span] = value[:main_rows]
            leaving(chunk).start()
            for j in range(pieces):
                q = chunk * pieces + j
                stack_ref[q * groups : (q + 1) * groups, :] = value[
                    main_rows:, j * piece : (j + 1) * piece
                ]
            if chunk == steps - 1:
                out_ref[:, half : half + piece] = lax.dot_general(
                    shuffle(main_rows, groups),
                    stack_ref[...],
                    (((0,), (0,)), ((), ())),
                    preferred_element_type=F32,
                ).astype(BF16)
                if cap is not None:
                    given().wait()
                    side_in = jnp.dot(
                        pick(groups, main_rows, 0, 0), given_ref[...], preferred_element_type=F32
                    )
                    out_ref[:, half + piece :] = make_side(
                        cap,
                        own_ref[...],
                        du1[rows:, :LANES].astype(F32),
                        side_in,
                        base_ref[...],
                        main_rows,
                    )
                leaving(steps).start()
                for number in range(steps + 1):
                    leaving(number).wait()


def backward_call(cap, head, grads, weights, crossed, *side):
    dg = grads[0]
    hidden = dg.shape[1]
    half = weights[0].shape[0] // 2
    span = 512
    steps = half // span
    rows = dg.shape[0]
    main_rows = rows // (MAIN + 1) * MAIN
    lanes = half + half // MAIN + (0 if cap is None else LANES)
    fixed = lambda i, head_ref: (0, 0)
    here = lambda i, head_ref: (head_ref[0] * steps + i, 0)
    anywhere = pl.BlockSpec(memory_space=pl.ANY)
    side_specs = [pl.BlockSpec(x.shape, fixed) for x in side[:-1]] + [anywhere] * len(side[-1:])
    side_scratch = [] if cap is None else [pltpu.VMEM((main_rows, LANES), BF16)]
    return pl.pallas_call(
        functools.partial(backward_kernel, span, steps, cap),
        grid_spec=pltpu.PrefetchScalarGridSpec(
            num_scalar_prefetch=1,
            grid=(steps,),
            in_specs=[pl.BlockSpec(x.shape, fixed) for x in grads]
            + [pl.BlockSpec((span, hidden), here)] * 4
            + side_specs,
            out_specs=anywhere,
            scratch_shapes=[
                pltpu.VMEM((main_rows, lanes), BF16),
                pltpu.VMEM((main_rows, half // MAIN), BF16),
                pltpu.SemaphoreType.DMA((steps + 2,)),
                *side_scratch,
            ],
        ),
        out_shape=jax.ShapeDtypeStruct((main_rows, lanes), BF16),
        compiler_params=pltpu.CompilerParams(
            dimension_semantics=("arbitrary",), vmem_limit_bytes=62 << 20
        ),
    )(head, *grads, *weights, *crossed, *side)


def first_rows_kernel(head_ref, ids_ref, tok_ref, out_ref, slot_ref, buf_ref, stack_ref, sem):
    toks, half = tok_ref.shape
    experts = slot_ref.shape[0]
    rows = out_ref.shape[0]
    piece = half // MAIN
    numbers = lax.broadcasted_iota(jnp.int32, (experts, toks), 0)
    hits = jnp.zeros((experts, toks), F32)
    for k in range(ids_ref.shape[0]):
        hits = jnp.where(ids_ref[k : k + 1, :] == numbers, 1.0, hits)
    a = lax.broadcasted_iota(jnp.int32, (toks, toks), 0)
    b = lax.broadcasted_iota(jnp.int32, (toks, toks), 1)
    before = jnp.dot(hits.astype(BF16), (a < b).astype(BF16), preferred_element_type=F32)
    slot = jnp.where(hits > 0.0, before, -1.0)
    slot_ref[...] = slot
    a = lax.broadcasted_iota(jnp.int32, (rows, experts), 0)
    b = lax.broadcasted_iota(jnp.int32, (rows, experts), 1)
    spread = ((a >= b * MAIN) & (a < b * MAIN + MAIN)).astype(BF16)
    slot_rows = jnp.dot(spread, slot.astype(BF16), preferred_element_type=F32)
    place = lax.broadcasted_iota(jnp.int32, (rows, toks), 0) % MAIN
    main = (slot_rows == place.astype(F32)).astype(BF16)
    in_extra = (slot == float(2 * MAIN)).astype(BF16)
    copies = []
    for q in range(MAIN + 1):
        cols = slice(q * piece, (q + 1) * piece)
        if q < MAIN:
            buf_ref[:, cols] = jnp.dot(
                main, tok_ref[:, cols], preferred_element_type=F32
            ).astype(BF16)
            stack_ref[q * experts : (q + 1) * experts, :] = jnp.dot(
                in_extra, tok_ref[:, cols], preferred_element_type=F32
            ).astype(BF16)
        else:
            dims = (((0,), (0,)), ((), ()))
            buf_ref[:, cols] = lax.dot_general(
                shuffle(rows, experts), stack_ref[...], dims, preferred_element_type=F32
            ).astype(BF16)
        copies.append(pltpu.make_async_copy(buf_ref.at[:, cols], out_ref.at[:, cols], sem.at[q]))
        copies[-1].start()
    for copy in copies:
        copy.wait()


def first_rows(head, ids, tokens, experts):
    toks, width = tokens.shape
    half = width // 2
    rows = experts * MAIN
    lanes = half + half // MAIN
    whole = lambda i, head_ref: (0, 0)
    return pl.pallas_call(
        first_rows_kernel,
        grid_spec=pltpu.PrefetchScalarGridSpec(
            num_scalar_prefetch=1,
            grid=(1,),
            in_specs=[
                pl.BlockSpec(ids.shape, whole),
                pl.BlockSpec((toks, half), lambda i, head_ref: (0, head_ref[0])),
            ],
            out_specs=[
                pl.BlockSpec(memory_space=pl.ANY),
                pl.BlockSpec((experts, toks), whole),
            ],
            scratch_shapes=[
                pltpu.VMEM((rows, lanes), BF16),
                pltpu.VMEM((rows, half // MAIN), BF16),
                pltpu.SemaphoreType.DMA((MAIN + 1,)),
            ],
        ),
        out_shape=[
            jax.ShapeDtypeStruct((rows, lanes), BF16),
            jax.ShapeDtypeStruct((experts, toks), F32),
        ],
        compiler_params=pltpu.CompilerParams(vmem_limit_bytes=60 << 20),
    )(head, ids, tokens)


def combiner(home_ref, slot_te, prob_te, first, extra_slot):
    rows = home_ref.shape[0]
    toks, experts = slot_te.shape
    half = home_ref.shape[1] // (LANES * (MAIN + 1)) * LANES * MAIN
    piece = half // MAIN
    a = lax.broadcasted_iota(jnp.int32, (experts, rows), 0)
    b = lax.broadcasted_iota(jnp.int32, (experts, rows), 1)
    spread = ((b >= a * MAIN) & (b < a * MAIN + MAIN)).astype(BF16)
    column = lax.broadcasted_iota(jnp.int32, (toks, rows), 1) % MAIN

    def repeat(x):
        return jnp.dot(x.astype(BF16), spread, preferred_element_type=F32)

    slot = repeat(slot_te)
    high = prob_te.astype(BF16)
    parts = (repeat(high), repeat(prob_te - high.astype(F32)))
    in_main = slot == (column + first).astype(F32)
    in_extra = slot == float(extra_slot)
    main = [jnp.where(in_main, p, 0.0).astype(BF16) for p in parts]

    def block(index):
        lo = index * 2 * piece
        rows_main = home_ref[:, lo : lo + 2 * piece]
        out = sum(jnp.dot(m, rows_main, preferred_element_type=F32) for m in main)
        extra = home_ref[:, half : half + piece]
        sides = []
        for q in (2 * index, 2 * index + 1):
            here = in_extra & (column == q)
            sides.append(
                sum(
                    jnp.dot(
                        jnp.where(here, p, 0.0).astype(BF16), extra, preferred_element_type=F32
                    )
                    for p in parts
                )
            )
        return out + jnp.concatenate(sides, axis=1)

    return block, 2 * piece


def first_combine_kernel(home_ref, slot_ref, prob_ref, line_ref, out_ref):
    block, width = combiner(home_ref, slot_ref[...], prob_ref[...], 0, 2 * MAIN)
    for i in range(out_ref.shape[1] // width):
        cols = slice(i * width, (i + 1) * width)
        out_ref[:, cols] = block(i) + line_ref[:, cols]


def fit_line(values, seq_lengths):
    n = float(values.shape[1])
    s1 = jnp.sum(seq_lengths, axis=1, keepdims=True)
    s2 = jnp.sum(seq_lengths * seq_lengths, axis=1, keepdims=True)
    v0 = jnp.sum(values, axis=1, keepdims=True)
    v1 = jnp.sum(values * seq_lengths, axis=1, keepdims=True)
    slope = (n * v1 - s1 * v0) / (n * s2 - s1 * s1)
    offset = (v0 - slope * s1) / n
    return values - offset - slope * seq_lengths


def last_combine_kernel(
    cap,
    home_ref,
    slot_ref,
    prob_ref,
    slot_et_ref,
    prob_et_ref,
    acc_ref,
    router_ref,
    lens_ref,
    pairs_ref,
    member_ref,
    out_ref,
):
    rows = home_ref.shape[0]
    experts = rows // MAIN
    seqs = lens_ref.shape[1]
    lines = seqs // LANES
    side = home_ref[:, home_ref.shape[1] - LANES :]
    chosen = pick(experts, rows, 3 * lines, 0)
    packed = jnp.dot(chosen, side, preferred_element_type=F32)
    score_es = join_pieces(packed, cap)
    slot_et = slot_et_ref[...]
    prob_et = prob_et_ref[...]
    score_et = jnp.zeros_like(prob_et)
    for c, number in enumerate(slot_order()):
        score_et = score_et + jnp.where(slot_et == float(number), score_es[:, c : c + 1], 0.0)
    mean_score = jnp.sum(prob_et * score_et, axis=0, keepdims=True)
    dlogits = (prob_et * (score_et - mean_score)).astype(BF16)
    totals = jnp.sum(side.astype(F32).reshape(experts, MAIN, LANES), axis=0)
    totals = totals[:lines] + totals[lines : 2 * lines] + totals[2 * lines : 3 * lines]
    reward = jnp.concatenate([totals[i : i + 1] for i in range(lines)], axis=1)
    lens = lens_ref[...]
    residual = fit_line(reward, lens)
    numbers = lax.broadcasted_iota(jnp.int32, (pairs_ref.shape[0], seqs), 1)
    delta = (numbers == pairs_ref[:, 0:1]).astype(F32) - (numbers == pairs_ref[:, 1:2]).astype(F32)
    margin = jnp.sum(delta * residual, axis=1, keepdims=True)
    pull = LOSS_SCALE / (1.0 + jnp.exp(margin))
    reward_grad = -jnp.sum(pull * delta, axis=0, keepdims=True)
    grad_back = fit_line(reward_grad, lens)
    coef = jnp.sum(member_ref[...] * grad_back, axis=1, keepdims=True)

    block, width = combiner(home_ref, slot_ref[...], prob_ref[...], MAIN, 2 * MAIN + 1)
    for i in range(out_ref.shape[1] // width):
        cols = slice(i * width, (i + 1) * width)
        router_term = lax.dot_general(
            dlogits, router_ref[:, cols], (((0,), (0,)), ((), ())), preferred_element_type=F32
        )
        out_ref[:, cols] = (coef * (block(i) + acc_ref[:, cols] + router_term)).astype(BF16)


def expand(extra_mask, pieces):
    experts, toks = extra_mask.shape
    eye = jnp.eye(pieces, dtype=extra_mask.dtype)
    full = extra_mask[:, None, None, :] * eye[None, :, :, None]
    return full.reshape(experts * pieces, pieces * toks)


def per_device(
    tokens,
    router_weight,
    gate_weight,
    up_weight,
    down_weight,
    head_weight,
    expert_ids,
    lengths,
    pairs,
):
    toks, width = tokens.shape
    experts = router_weight.shape[1]
    groups = lengths.shape[0]
    seq_dev = lengths.shape[1]
    seqs = groups * seq_dev
    half = width // 2
    piece = half // MAIN
    cap = 2 * (MAIN + 1)
    me = lax.axis_index("expert")
    head = lax.axis_index("head")
    w_gate, w_up, w_down = gate_weight[0], up_weight[0], down_weight[0]

    main_rows = groups * MAIN
    head_number = head.astype(jnp.int32)[None]
    block_a, slot_ef = first_rows(head_number, expert_ids.T, tokens, experts)
    slot_te = slot_ef.T
    recv_a = exchange(block_a.reshape(experts, MAIN, -1))
    hits = slot_te >= 0.0
    slot_et = slot_ef.astype(jnp.int32)

    def masks(first, extra):
        slots = first + jnp.arange(MAIN, dtype=jnp.int32)
        main = (slot_et[:, None, :] == slots[None, :, None]).astype(BF16)
        return main.reshape(experts * MAIN, toks), (slot_et == extra).astype(BF16)

    mask_b = masks(MAIN, 2 * MAIN + 1)
    tok_half = lax.dynamic_slice_in_dim(tokens, head * half, half, 1)
    tok_pieces = tok_half.reshape(toks, MAIN, piece).transpose(1, 0, 2).reshape(MAIN * toks, piece)

    def gather_rows(mask):
        main = jnp.dot(mask[0], tok_half, preferred_element_type=F32).astype(BF16)
        extra = jnp.dot(expand(mask[1], MAIN), tok_pieces, preferred_element_type=F32).astype(BF16)
        return jnp.concatenate(
            [main.reshape(experts, MAIN, half), extra.reshape(experts, MAIN, piece)], axis=2
        )


    logits = jnp.dot(tokens, router_weight, preferred_element_type=F32)
    masked = jnp.where(hits, logits, -jnp.inf)
    top = jnp.max(masked, axis=1, keepdims=True)
    weights = jnp.where(hits, jnp.exp(logits - top), 0.0)
    prob = weights / jnp.sum(weights, axis=1, keepdims=True)
    own_lengths = lax.dynamic_slice_in_dim(lengths, me, 1, 0)[0]
    ends = jnp.cumsum(own_lengths)
    starts = ends - own_lengths
    position = jnp.arange(toks, dtype=jnp.int32)[:, None]
    member = ((position >= starts[None, :]) & (position < ends[None, :])).astype(F32)
    own_float = own_lengths.astype(F32)
    seq_of = jnp.sum(member * jnp.arange(seq_dev, dtype=F32)[None, :], axis=1)
    inv_len = jnp.sum(member / own_float[None, :], axis=1)

    slot_iota = jnp.array(slot_order(), jnp.int32)
    at_slot = slot_et[:, None, :] == slot_iota[None, :, None]
    weight_et = (prob * inv_len[:, None]).T
    weight_slot = jnp.sum(jnp.where(at_slot, weight_et[:, None, :], 0.0), axis=2)
    seq_slot = jnp.sum(jnp.where(at_slot, seq_of[None, None, :], 0.0), axis=2)
    side = jnp.concatenate([*split_three(weight_slot), seq_slot.astype(BF16)], axis=1)
    side = jnp.pad(side, ((0, 0), (0, LANES - 4 * cap)))
    side = jnp.pad(side[:, None, :], ((0, 0), (0, MAIN - 1), (0, 0)))
    block_b = jnp.concatenate([gather_rows(mask_b), side], axis=2)
    recv_b = exchange(block_b)

    head_map = jnp.dot(w_down, head_weight, preferred_element_type=F32)
    base = jnp.dot(tokens, head_weight, preferred_element_type=F32)
    base_reward = jnp.sum(base[:, None] * member, axis=0) / own_float

    head_line = head_map[None, :]

    weights = (w_gate, w_up)
    crossed = [swap(w) for w in weights]

    def forward(cap, recv, before, after):
        own = recv.reshape(main_rows, -1)
        other = swap(recv).reshape(main_rows, -1)
        return forward_call(cap, head_number, own, other, *weights, head_line, before, after)

    own_row = jnp.arange(groups, dtype=jnp.int32)[:, None] == me
    base_line = jnp.where(own_row, base_reward[None, :], 0.0).reshape(1, seqs)
    recv_a = touch(recv_a, block_b, head_line, base_line, *crossed)
    dg_a, du_a, score_a = forward(None, recv_a, head_line, head_line)
    grads_a = (dg_a, du_a, swap(dg_a), swap(du_a))
    total_a = backward_call(None, head_number, grads_a, weights, crossed)
    recv_b = touch(recv_b, total_a)
    home_a = exchange(total_a.reshape(groups, MAIN, -1))
    dg_b, du_b, score_b = forward(cap, recv_b, score_a, total_a)
    grads_b = (dg_b, du_b, swap(dg_b), swap(du_b))
    total_b = backward_call(
        cap,
        head_number,
        grads_b,
        weights,
        crossed,
        score_b,
        base_line,
        recv_b.reshape(main_rows, -1),
    )
    total_b = touch(total_b, home_a)
    home_b = exchange(total_b.reshape(groups, MAIN, -1))

    head_half = lax.dynamic_slice_in_dim(head_weight, head * half, half, 0).astype(F32)[None, :]
    acc = pl.pallas_call(
        first_combine_kernel,
        out_shape=jax.ShapeDtypeStruct((toks, half), F32),
        compiler_params=pltpu.CompilerParams(vmem_limit_bytes=24 << 20),
    )(home_a.reshape(main_rows, -1), slot_te, prob, head_half)

    router_half = lax.dynamic_slice_in_dim(router_weight, head * half, half, 0).T
    own_seq = me * seq_dev + jnp.arange(seq_dev, dtype=jnp.int32)
    places = (jnp.arange(seqs, dtype=jnp.int32)[None, :] == own_seq[:, None]).astype(F32)
    member_line = jnp.sum((member / own_float[None, :])[:, :, None] * places[None], axis=1)
    return pl.pallas_call(
        functools.partial(last_combine_kernel, cap),
        out_shape=jax.ShapeDtypeStruct((toks, half), BF16),
        in_specs=[pl.BlockSpec(memory_space=pltpu.VMEM)] + [pl.BlockSpec()] * 9,
        compiler_params=pltpu.CompilerParams(vmem_limit_bytes=24 << 20),
    )(
        home_b.reshape(main_rows, -1),
        slot_te,
        prob,
        slot_ef,
        prob.T,
        acc,
        router_half,
        lengths.astype(F32).reshape(1, seqs),
        pairs,
        member_line,
    )


def solution(mesh):
    return jax.shard_map(
        per_device,
        mesh=mesh,
        in_specs=(
            P("expert", None),
            P(),
            P("expert", None, "head"),
            P("expert", None, "head"),
            P("expert", "head", None),
            P(),
            P("expert", None),
            P(),
            P(),
        ),
        out_specs=P("expert", "head"),
        check_vma=False,
    )
```

profile of v0, /device:TPU:0, one launch (start us, length us, event | category | flops | bytes accessed | tf_op | source)
XLA Modules:
  0.0 184.2 jit_solution(17659911189214808859)
XLA Ops:
  0.0 0.5 collective-permute-start.1
  0.5 3.8 %shard_map.100 = (bf16[512,2304]{1,0:T(8,128)(2,1)}, f32[64,128]{1,0:T(8,128)}) custom-call(s32[1]{0:T(128)} %bitcast.head_ref, s32[8,128]{1,0:T(8,128)} %bitcast.88, bf16[128,4096]{1,0:T(8,128)(2,1)} %tok_ref.1), custom_call_target="tpu_custom_call" | custom-call | tf_op jit(solution)/shard_map/pallas_call | solution.py:441
  4.4 11.6 %all-to-all-start.1 = ((bf16[64,8,2304]{2,1,0:T(8,128)(2,1)}), bf16[64,8,2304]{2,1,0:T(8,128)(2,1)S(1)}, u32[]{:S(2)}, u32[]{:S(2)}) async-start(bf16[64,8,2304]{2,1,0:T(8,128)(2,1)} %bitcast.85), calls=%async_computation.1 | async-start | bytes 4718592 | tf_op jit(solution)/shard_map/all_to_all | solution.py:26
  16.1 0.1 copy.53
  16.2 0.2 reduce-window.4
  16.5 0.7 eq.77
  17.2 1.7 select_reduce_fusion
  18.9 1.6 convolution_bitcast_fusion
  20.5 1.4 select_reduce_fusion.1
  21.9 0.5 fusion.8
  22.4 0.7 copy.43
  23.2 1.1 constant_dynamic-slice_fusion.1
  24.2 1.0 copy.52
  25.2 2.1 %copy.40 = bf16[8,128,256]{2,1,0:T(8,128)(2,1)} copy(bf16[8,128,256]{1,2,0:T(8,128)(2,1)} %bitcast.86) | data formatting | bytes 1048576 | tf_op jit(solution)/shard_map/transpose | solution.py:623
  27.3 0.7 fusion.29
  28.0 0.7 broadcast_select_fusion
  28.7 1.4 select_n.49.refs_3_.refs_9_
  30.2 1.5 fusion.3
  31.7 0.1 multiply_bitcast_fusion
  31.8 0.4 fusion.5
  32.3 1.7 fusion.4.refs_1_
  33.9 5.1 %fusion.refs_2_.hm_ref.before_ref.after_ref = f32[1,768]{1,0:T(1,128)} fusion(bf16[4096,1]{0,1:T(2,128)(2,1)S(1)} %reshape.216, bf16[1,768,4096]{2,1,0:T(8,128)(2,1)} %param.14), kind=kOutput, calls=%fused_computation | convolution fusion | flops 6291456 | bytes 6302720 | tf_op jit(solution)/shard_map/dot_general | solution.py:658
  39.0 9.6 %all-to-all-done.1.refs_0_ = bf16[64,8,2304]{2,1,0:T(8,128)(2,1)S(1)} async-done(((bf16[64,8,2304]{2,1,0:T(8,128)(2,1)}), bf16[64,8,2304]{2,1,0:T(8,128)(2,1)S(1)}, u32[]{:S(2)}, u32[]{:S(2)}) %all-to-all-start.1) | async-done | bytes 2359328 | tf_op jit(solution)/shard_map/all_to_all | solution.py:26
  48.6 1.5 copy-done.2
  50.1 6.4 %all-to-all-start = ((bf16[64,8,2432]{2,1,0:T(8,128)(2,1)}), bf16[64,8,2432]{2,1,0:T(8,128)(2,1)}, u32[]{:S(2)}, u32[]{:S(2)}) async-start(bf16[64,8,2432]{2,1,0:T(8,128)(2,1)} %fusion.4.refs_1_), calls=%async_computation | async-start | bytes 4980736 | tf_op jit(solution)/shard_map/all_to_all | solution.py:26
  56.5 16.0 %shard_map.102 = (bf16[576,768]{1,0:T(8,128)(2,1)}, bf16[576,768]{1,0:T(8,128)(2,1)}, f32[64,128]{1,0:T(8,128)}) custom-call(s32[1]{0:T(128)} %bitcast.head_ref, bf16[512,2304]{1,0:T(8,128)(2,1)} %bitcast.84, bf16[512,2304]{1,0:T(8,128)(2,1)} %bitcast.24.other_hbm, bf16[4096,768]{1,0:T(8,128)(2,1)} %bitcast.74, bf16[4096,768]{1,0:T(8,128)(2,1)} %bitcast.79, ...), custom_call_target="tpu_custom_call" | custom-call | tf_op jit(solution)/shard_map/pallas_call | solution.py:220
  72.5 0.4 collective-permute-start.3
  72.9 0.2 collective-permute-start.4
  73.1 2.1 %collective-permute-done.3.refs_2_ = bf16[576,768]{1,0:T(8,128)(2,1)S(1)} collective-permute-done((bf16[576,768]{1,0:T(8,128)(2,1)}, bf16[576,768]{1,0:T(8,128)(2,1)S(1)}, u32[]{:S(2)}, u32[]{:S(2)}) %collective-permute-start.3) | collective-permute-done | bytes 884768 | tf_op jit(solution)/shard_map/ppermute | solution.py:30
  75.2 1.4 collective-permute-done.4.refs_3_
  76.6 12.5 %shard_map.103.refs_1_.after_ref = bf16[512,2304]{1,0:T(8,128)(2,1)} custom-call(s32[1]{0:T(128)} %bitcast.head_ref, bf16[576,768]{1,0:T(8,128)(2,1)} %get-tuple-element.15.refs_0_, bf16[576,768]{1,0:T(8,128)(2,1)} %get-tuple-element.16.refs_1_, bf16[576,768]{1,0:T(8,128)(2,1)} %copy-done.5, bf16[576,768]{1,0:T(8,128)(2,1)} %collective-permute-done.4.refs_3_, ...), custom_call_target="tpu_custom_call" | custom-call | tf_op jit(solution)/shard_map/pallas_call | solution.py:370
  89.2 1.2 all-to-all-done.refs_0_
  90.4 9.6 %all-to-all-start.2 = ((bf16[64,8,2304]{2,1,0:T(8,128)(2,1)}), bf16[64,8,2304]{2,1,0:T(8,128)(2,1)}, u32[]{:S(2)}, u32[]{:S(2)}) async-start(bf16[64,8,2304]{2,1,0:T(8,128)(2,1)} %bitcast.27), calls=%async_computation.2 | async-start | bytes 4718592 | tf_op jit(solution)/shard_map/all_to_all | solution.py:26
  100.0 15.8 %shard_map.105 = (bf16[576,768]{1,0:T(8,128)(2,1)}, bf16[640,768]{1,0:T(8,128)(2,1)}, f32[64,128]{1,0:T(8,128)}) custom-call(s32[1]{0:T(128)} %bitcast.head_ref, bf16[512,2432]{1,0:T(8,128)(2,1)} %bitcast.25.own_hbm.refs_10_, bf16[512,2432]{1,0:T(8,128)(2,1)} %bitcast.26.other_hbm, bf16[4096,768]{1,0:T(8,128)(2,1)} %bitcast.76, bf16[4096,768]{1,0:T(8,128)(2,1)} %bitcast.81, ...), custom_call_target="tpu_custom_call" | custom-call | tf_op jit(solution)/shard_map/pallas_call | solution.py:220
  115.8 0.2 collective-permute-start.7
  116.0 0.4 collective-permute-start.6
  116.4 3.5 %collective-permute-done.6.refs_2_ = bf16[576,768]{1,0:T(8,128)(2,1)S(1)} collective-permute-done((bf16[576,768]{1,0:T(8,128)(2,1)}, bf16[576,768]{1,0:T(8,128)(2,1)S(1)}, u32[]{:S(2)}, u32[]{:S(2)}) %collective-permute-start.6) | collective-permute-done | bytes 884768 | tf_op jit(solution)/shard_map/ppermute | solution.py:30
  119.9 1.0 copy-done.4
  121.0 0.9 copy-done.3
  121.9 13.2 %shard_map.106.refs_0_ = bf16[512,2432]{1,0:T(8,128)(2,1)} custom-call(s32[1]{0:T(128)} %bitcast.head_ref, bf16[576,768]{1,0:T(8,128)(2,1)} %get-tuple-element.18.refs_0_, bf16[640,768]{1,0:T(8,128)(2,1)} %get-tuple-element.19.refs_1_, bf16[576,768]{1,0:T(8,128)(2,1)} %copy-done.4, bf16[640,768]{1,0:T(8,128)(2,1)} %copy-done.3, bf16[4096,768]{1,0:T(8,128)(2,1)} %bitcast.77, ...), custom_call_target="tpu_custom_call" | custom-call | tf_op jit(solution)/shard_map/pallas_call | solution.py:370
  135.2 10.6 %all-to-all-start.3 = ((bf16[64,8,2432]{2,1,0:T(8,128)(2,1)}), bf16[64,8,2432]{2,1,0:T(8,128)(2,1)}, u32[]{:S(2)}, u32[]{:S(2)}) async-start(bf16[64,8,2432]{2,1,0:T(8,128)(2,1)} %bitcast.83), calls=%async_computation.3 | async-start | bytes 4980736 | tf_op jit(solution)/shard_map/all_to_all | solution.py:26
  146.1 0.1 copy.49.pairs_ref
  146.2 0.1 copy.46
  146.3 0.1 reshape.214.lens_ref
  146.5 0.1 multiply_reduce_fusion.member_ref
  146.7 3.4 %shard_map.108.acc_ref = f32[128,2048]{1,0:T(8,128)S(1)} custom-call(bf16[512,2304]{1,0:T(8,128)(2,1)} %bitcast.30.home_ref, f32[128,64]{1,0:T(8,128)S(1)} %copy.47.slot_ref, f32[128,64]{1,0:T(8,128)S(1)} %copy.48.prob_ref, f32[1,2048]{1,0:T(1,128)S(1)} %bitcast.72), custom_call_target="tpu_custom_call" | custom-call | tf_op jit(solution)/shard_map/pallas_call | solution.py:696
  150.1 29.3 %all-to-all-done.3 = bf16[64,8,2432]{2,1,0:T(8,128)(2,1)} async-done(((bf16[64,8,2432]{2,1,0:T(8,128)(2,1)}), bf16[64,8,2432]{2,1,0:T(8,128)(2,1)}, u32[]{:S(2)}, u32[]{:S(2)}) %all-to-all-start.3) | async-done | bytes 2490400 | tf_op jit(solution)/shard_map/all_to_all | solution.py:26
  179.4 4.8 %shard_map.109 = bf16[128,2048]{1,0:T(8,128)(2,1)} custom-call(bf16[512,2432]{1,0:T(8,128)(2,1)} %bitcast.29.home_ref, f32[128,64]{1,0:T(8,128)S(1)} %copy.47.slot_ref, f32[128,64]{1,0:T(8,128)S(1)} %copy.48.prob_ref, f32[64,128]{1,0:T(8,128)S(1)} %copy-done.1, f32[64,128]{1,0:T(8,128)S(1)} %get-tuple-element.27.prob_et_ref, ...), custom_call_target="tpu_custom_call" | custom-call | tf_op jit(solution)/shard_map/pallas_call | solution.py:706
  (73 shorter events, 0.6 us)
Async XLA Ops:
  0.0 17.2 %copy-start = (bf16[4096,64]{0,1:T(8,128)(2,1)S(1)}, bf16[4096,64]{0,1:T(8,128)(2,1)}, u32[]{:S(2)}) copy-start(bf16[4096,64]{0,1:T(8,128)(2,1)} %param.11) | copy-start | bytes 1572868
  0.0 48.6 %collective-permute-start = (bf16[4096,768]{1,0:T(8,128)(2,1)}, bf16[4096,768]{1,0:T(8,128)(2,1)}, u32[]{:S(2)}, u32[]{:S(2)}) collective-permute-start(bf16[4096,768]{1,0:T(8,128)(2,1)} %bitcast.73), channel_id=1, source_target_pairs={{0,1},{1,0},{2,3},{3,2},{4,5},{5,4},{6,7},{7,6},{8,9},{9,8},{10,11... | collective-permute-start | bytes 18874376 | tf_op jit(solution)/shard_map/ppermute | solution.py:30
  0.0 48.6 %collective-permute-start.1 = (bf16[4096,768]{1,0:T(8,128)(2,1)}, bf16[4096,768]{1,0:T(8,128)(2,1)}, u32[]{:S(2)}, u32[]{:S(2)}) collective-permute-start(bf16[4096,768]{1,0:T(8,128)(2,1)} %bitcast.78), channel_id=1, source_target_pairs={{0,1},{1,0},{2,3},{3,2},{4,5},{5,4},{6,7},{7,6},{8,9},{9,8},{10,11... | collective-permute-start | bytes 18874376 | tf_op jit(solution)/shard_map/ppermute | solution.py:30
  4.4 11.7 %copy-start.15 = (s32[64,4]{0,1:T(4,128)S(1)}, s32[64,4]{0,1:T(4,128)}, u32[]{:S(2)}) copy-start(s32[64,4]{0,1:T(4,128)} %param.17) | copy-start | bytes 3076
  4.4 12.1 %copy-start.10 = (bf16[4096]{0:T(1024)(128)(2,1)S(1)}, bf16[4096]{0:T(1024)(128)(2,1)}, u32[]{:S(2)}) copy-start(bf16[4096]{0:T(1024)(128)(2,1)} %param.15) | copy-start | bytes 24580
  4.4 12.8 %copy-start.1 = (f32[64,128]{1,0:T(8,128)S(1)}, f32[64,128]{1,0:T(8,128)}, u32[]{:S(2)}) copy-start(f32[64,128]{1,0:T(8,128)} %get-tuple-element.13.slot_et_ref) | copy-start | bytes 98308
  4.4 44.2 %all-to-all-start.1 = ((bf16[64,8,2304]{2,1,0:T(8,128)(2,1)}), bf16[64,8,2304]{2,1,0:T(8,128)(2,1)S(1)}, u32[]{:S(2)}, u32[]{:S(2)}) async-start(bf16[64,8,2304]{2,1,0:T(8,128)(2,1)} %bitcast.85), calls=%async_computation.1 | async-start | bytes 4718592 | tf_op jit(solution)/shard_map/all_to_all | solution.py:26
  16.0 5.9 %copy-start.21 = (s32[18]{0:T(128)S(1)}, s32[18]{0:T(128)}, u32[]{:S(2)}) copy-start(s32[18]{0:T(128)} %constant.36.clone) | copy-start | bytes 220
  16.2 5.7 %copy-start.19 = (s32[1,4]{1,0:T(1,128)}, s32[1,4]{1,0:T(1,128)S(1)}, u32[]{:S(2)}) copy-start(s32[1,4]{1,0:T(1,128)S(1)} %copy.53) | copy-start | bytes 52
  18.9 3.0 %copy-start.8 = (pred[128,64]{0,1:T(8,128)(4,1)}, pred[128,64]{0,1:T(8,128)(4,1)S(1)}, u32[]{:S(2)}) copy-start(pred[128,64]{0,1:T(8,128)(4,1)S(1)} %get-tuple-element.29) | copy-start | bytes 24580
  18.9 3.0 %copy-start.12 = (f32[128]{0:T(128)}, f32[128]{0:T(128)S(1)}, u32[]{:S(2)}) copy-start(f32[128]{0:T(128)S(1)} %get-tuple-element.28) | copy-start | bytes 1540
  18.9 3.0 %copy-start.17 = (f32[128]{0:T(128)}, f32[128]{0:T(128)S(1)}, u32[]{:S(2)}) copy-start(f32[128]{0:T(128)S(1)} %fusion.23) | copy-start | bytes 1540
  30.1 1.7 copy-start.6
  30.1 2.1 %copy-start.7 = (bf16[64,1,128]{2,1,0:T(2,128)(2,1)S(1)}, bf16[64,1,128]{2,1,0:T(2,128)(2,1)}, u32[]{:S(2)}) copy-start(bf16[64,1,128]{2,1,0:T(2,128)(2,1)} %copy.43) | copy-start | bytes 49156
  48.6 1.5 copy-start.2
  50.1 6.4 %collective-permute-start.2 = (bf16[64,8,2304]{2,1,0:T(8,128)(2,1)}, bf16[64,8,2304]{2,1,0:T(8,128)(2,1)}, u32[]{:S(2)}, u32[]{:S(2)}) collective-permute-start(bf16[64,8,2304]{2,1,0:T(8,128)(2,1)} %shard_map.101), channel_id=1, source_target_pairs={{0,1},{1,0},{2,3},{3,2},{4,5},{5,4},{6,7},{7,6},{8,9},{9,8},{10,11... | collective-permute-start | bytes 7077896 | tf_op jit(solution)/shard_map/ppermute | solution.py:30
  50.1 40.3 %all-to-all-start = ((bf16[64,8,2432]{2,1,0:T(8,128)(2,1)}), bf16[64,8,2432]{2,1,0:T(8,128)(2,1)}, u32[]{:S(2)}, u32[]{:S(2)}) async-start(bf16[64,8,2432]{2,1,0:T(8,128)(2,1)} %fusion.4.refs_1_), calls=%async_computation | async-start | bytes 4980736 | tf_op jit(solution)/shard_map/all_to_all | solution.py:26
  72.5 2.7 %collective-permute-start.3 = (bf16[576,768]{1,0:T(8,128)(2,1)}, bf16[576,768]{1,0:T(8,128)(2,1)S(1)}, u32[]{:S(2)}, u32[]{:S(2)}) collective-permute-start(bf16[576,768]{1,0:T(8,128)(2,1)} %get-tuple-element.15.refs_0_), channel_id=1, source_target_pairs={{0,1},{1,0},{2,3},{3,2},{4,5},{5,4},{6,7},{7,6},{8,9},{9,8},{10,11... | collective-permute-start | bytes 2654216 | tf_op jit(solution)/shard_map/ppermute | solution.py:30
  72.9 3.8 %collective-permute-start.4 = (bf16[576,768]{1,0:T(8,128)(2,1)}, bf16[576,768]{1,0:T(8,128)(2,1)}, u32[]{:S(2)}, u32[]{:S(2)}) collective-permute-start(bf16[576,768]{1,0:T(8,128)(2,1)} %get-tuple-element.16.refs_1_), channel_id=1, source_target_pairs={{0,1},{1,0},{2,3},{3,2},{4,5},{5,4},{6,7},{7,6},{8,9},{9,8},{10,11... | collective-permute-start | bytes 2654216 | tf_op jit(solution)/shard_map/ppermute | solution.py:30
  75.2 1.4 copy-start.5
  90.4 9.6 %collective-permute-start.5 = (bf16[64,8,2432]{2,1,0:T(8,128)(2,1)}, bf16[64,8,2432]{2,1,0:T(8,128)(2,1)}, u32[]{:S(2)}, u32[]{:S(2)}) collective-permute-start(bf16[64,8,2432]{2,1,0:T(8,128)(2,1)} %shard_map.104), channel_id=1, source_target_pairs={{0,1},{1,0},{2,3},{3,2},{4,5},{5,4},{6,7},{7,6},{8,9},{9,8},{10,11... | collective-permute-start | bytes 7471112 | tf_op jit(solution)/shard_map/ppermute | solution.py:30
  90.4 44.8 %all-to-all-start.2 = ((bf16[64,8,2304]{2,1,0:T(8,128)(2,1)}), bf16[64,8,2304]{2,1,0:T(8,128)(2,1)}, u32[]{:S(2)}, u32[]{:S(2)}) async-start(bf16[64,8,2304]{2,1,0:T(8,128)(2,1)} %bitcast.27), calls=%async_computation.2 | async-start | bytes 4718592 | tf_op jit(solution)/shard_map/all_to_all | solution.py:26
  115.8 4.1 %collective-permute-start.7 = (bf16[640,768]{1,0:T(8,128)(2,1)}, bf16[640,768]{1,0:T(8,128)(2,1)S(1)}, u32[]{:S(2)}, u32[]{:S(2)}) collective-permute-start(bf16[640,768]{1,0:T(8,128)(2,1)} %get-tuple-element.19.refs_1_), channel_id=1, source_target_pairs={{0,1},{1,0},{2,3},{3,2},{4,5},{5,4},{6,7},{7,6},{8,9},{9,8},{10,11... | collective-permute-start | bytes 2949128 | tf_op jit(solution)/shard_map/ppermute | solution.py:30
  116.0 4.0 %collective-permute-start.6 = (bf16[576,768]{1,0:T(8,128)(2,1)}, bf16[576,768]{1,0:T(8,128)(2,1)S(1)}, u32[]{:S(2)}, u32[]{:S(2)}) collective-permute-start(bf16[576,768]{1,0:T(8,128)(2,1)} %get-tuple-element.18.refs_0_), channel_id=1, source_target_pairs={{0,1},{1,0},{2,3},{3,2},{4,5},{5,4},{6,7},{7,6},{8,9},{9,8},{10,11... | collective-permute-start | bytes 2654216 | tf_op jit(solution)/shard_map/ppermute | solution.py:30
  119.9 1.0 copy-start.4
  121.0 0.9 copy-start.3
  135.2 10.7 %copy-start.16 = (s32[64,4]{0,1:T(4,128)S(1)}, s32[64,4]{0,1:T(4,128)}, u32[]{:S(2)}) copy-start(s32[64,4]{0,1:T(4,128)} %param.17) | copy-start | bytes 3076
  135.2 10.7 %copy-start.9 = (pred[128,64]{0,1:T(8,128)(4,1)S(1)}, pred[128,64]{0,1:T(8,128)(4,1)}, u32[]{:S(2)}) copy-start(pred[128,64]{0,1:T(8,128)(4,1)} %copy-done.8) | copy-start | bytes 24580
  135.2 10.7 %copy-start.13 = (f32[128]{0:T(128)S(1)}, f32[128]{0:T(128)}, u32[]{:S(2)}) copy-start(f32[128]{0:T(128)} %copy-done.12) | copy-start | bytes 1540
  135.2 10.7 %copy-start.18 = (f32[128]{0:T(128)S(1)}, f32[128]{0:T(128)}, u32[]{:S(2)}) copy-start(f32[128]{0:T(128)} %copy-done.17) | copy-start | bytes 1540
  135.2 10.9 %copy-start.20 = (s32[128,2]{0,1:T(2,128)S(1)}, s32[128,2]{0,1:T(2,128)}, u32[]{:S(2)}) copy-start(s32[128,2]{0,1:T(2,128)} %param.18) | copy-start | bytes 3076
  135.2 11.2 %copy-start.11 = (bf16[4096]{0:T(1024)(128)(2,1)S(1)}, bf16[4096]{0:T(1024)(128)(2,1)}, u32[]{:S(2)}) copy-start(bf16[4096]{0:T(1024)(128)(2,1)} %param.15) | copy-start | bytes 24580
  135.2 11.3 %copy-start.14 = (f32[128,4]{0,1:T(4,128)S(1)}, f32[128,4]{0,1:T(4,128)}, u32[]{:S(2)}) copy-start(f32[128,4]{0,1:T(4,128)} %get-tuple-element.34) | copy-start | bytes 6148
  135.2 44.2 %all-to-all-start.3 = ((bf16[64,8,2432]{2,1,0:T(8,128)(2,1)}), bf16[64,8,2432]{2,1,0:T(8,128)(2,1)}, u32[]{:S(2)}, u32[]{:S(2)}) async-start(bf16[64,8,2432]{2,1,0:T(8,128)(2,1)} %bitcast.83), calls=%async_computation.3 | async-start | bytes 4980736 | tf_op jit(solution)/shard_map/all_to_all | solution.py:26
where the time goes:
time: 185 us; the launch traced here: 184 us
  Pallas kernels  69.7 us (38%)
  waiting for transfers between devices  47.1 us (25%)
  starting transfers between devices  39.9 us (22%)
  local copies, waits for them, and re-layouts  11.2 us (6%)
  matrix products  10.4 us (6%)
  other arithmetic  5.51 us (3%)
    all_to_all x4, waiting for transfers between devices, exchange(): return lax.all_to_all(x, 'expert', split_axis=0, concat_axis=0, tiled=True)  40.1 us
    all_to_all x4, starting transfers between devices, exchange(): return lax.all_to_all(x, 'expert', split_axis=0, concat_axis=0, tiled=True)  38.2 us
    pallas_call x2, Pallas kernels, forward_call(): pl.pallas_call(functools.partial(forward_kernel, span, steps, cap), grid_...  31.8 us
    pallas_call x2, Pallas kernels, backward_call(): pl.pallas_call(functools.partial(backward_kernel, span, steps, cap), grid...  25.8 us
    ppermute x8, waiting for transfers between devices, swap(): return lax.ppermute(x, 'head', SWAP)  7.06 us
    unnamed x49, local copies, waits for them, and re-layouts  5.8 us
    dot_general x1, matrix products, per_device(): head_map = jnp.dot(w_down, head_weight, preferred_element_type=F32)  5.11 us
    pallas_call x1, Pallas kernels, per_device(): pl.pallas_call(functools.partial(last_combine_kernel, cap), out_shape=jax...  4.83 us
  transfers between devices with their start and end apart: 12, of which 6 were waited for; matrix products, arithmetic and copies ran while one was open for 13% of the time, Pallas kernels for 35%

commit v1 on v0

--- a/solution.py
+++ b/solution.py
@@ -71,13 +71,14 @@
     pass
 
 
-def touch(x, *after):
+def touch(x, *after, limit=None):
     return pl.pallas_call(
         touch_kernel,
         out_shape=jax.ShapeDtypeStruct(x.shape, x.dtype),
         in_specs=[pl.BlockSpec(memory_space=pl.ANY)] * (1 + len(after)),
         out_specs=pl.BlockSpec(memory_space=pl.ANY),
         input_output_aliases={0: 0},
+        compiler_params=pltpu.CompilerParams(vmem_limit_bytes=limit),
     )(x, *after)
 
 
@@ -385,7 +386,7 @@
         ),
         out_shape=jax.ShapeDtypeStruct((main_rows, lanes), BF16),
         compiler_params=pltpu.CompilerParams(
-            dimension_semantics=("arbitrary",), vmem_limit_bytes=62 << 20
+            dimension_semantics=("arbitrary",), vmem_limit_bytes=60 << 20
         ),
     )(head, *grads, *weights, *crossed, *side)
 
@@ -482,25 +483,25 @@
     high = prob_te.astype(BF16)
     parts = (repeat(high), repeat(prob_te - high.astype(F32)))
     in_main = slot == (column + first).astype(F32)
-    in_extra = slot == float(extra_slot)
+    in_extra = slot_te == float(extra_slot)
     main = [jnp.where(in_main, p, 0.0).astype(BF16) for p in parts]
+
+    extra = [
+        jnp.where(in_extra, p, 0.0).astype(BF16)
+        for p in (high.astype(F32), prob_te - high.astype(F32))
+    ]
+    stack = jnp.dot(
+        shuffle(rows, experts), home_ref[:, half : half + piece], preferred_element_type=F32
+    ).astype(BF16)
 
     def block(index):
         lo = index * 2 * piece
         rows_main = home_ref[:, lo : lo + 2 * piece]
         out = sum(jnp.dot(m, rows_main, preferred_element_type=F32) for m in main)
-        extra = home_ref[:, half : half + piece]
         sides = []
         for q in (2 * index, 2 * index + 1):
-            here = in_extra & (column == q)
-            sides.append(
-                sum(
-                    jnp.dot(
-                        jnp.where(here, p, 0.0).astype(BF16), extra, preferred_element_type=F32
-                    )
-                    for p in parts
-                )
-            )
+            here = stack[q * experts : (q + 1) * experts]
+            sides.append(sum(jnp.dot(m, here, preferred_element_type=F32) for m in extra))
         return out + jnp.concatenate(sides, axis=1)
 
     return block, 2 * piece
@@ -653,7 +654,6 @@
     side = jnp.pad(side, ((0, 0), (0, LANES - 4 * cap)))
     side = jnp.pad(side[:, None, :], ((0, 0), (0, MAIN - 1), (0, 0)))
     block_b = jnp.concatenate([gather_rows(mask_b), side], axis=2)
-    recv_b = exchange(block_b)
 
     head_map = jnp.dot(w_down, head_weight, preferred_element_type=F32)
     base = jnp.dot(tokens, head_weight, preferred_element_type=F32)
@@ -671,7 +671,9 @@
 
     own_row = jnp.arange(groups, dtype=jnp.int32)[:, None] == me
     base_line = jnp.where(own_row, base_reward[None, :], 0.0).reshape(1, seqs)
-    recv_a = touch(recv_a, block_b, head_line, base_line, *crossed)
+    block_b = touch(block_b, head_line, base_line, limit=62 << 20)
+    recv_b = exchange(block_b)
+    recv_a = touch(recv_a, block_b, *crossed)
     dg_a, du_a, score_a = forward(None, recv_a, head_line, head_line)
     grads_a = (dg_a, du_a, swap(dg_a), swap(du_a))
     total_a = backward_call(None, head_number, grads_a, weights, crossed)

time: 185 us -> 183 us (0.989)
  waiting for transfers between devices: 47.1 us -> 57.9 us
  local copies, waits for them, and re-layouts: 11.2 us -> 4.4 us
  matrix products: 10.4 us -> 7.15 us
  other arithmetic: 5.51 us -> 3.07 us
    all_to_all x4, waiting for transfers between devices: 40.1 us -> 50.9 us  [exchange(): return lax.all_to_all(x, 'expert', split_axis=0, concat_axis=0, tiled=True)]
    unnamed x49 -> x27, local copies, waits for them, and re-layouts: 5.8 us -> 2.8 us
    transpose x1, local copies, waits for them, and re-layouts: 2.08 us -> 0.22 us  [per_device(): tok_half.reshape(toks, MAIN, piece).transpose(1, 0, 2)]
  transfers between devices with their start and end apart: 12 -> 12, of which waited for: 6 -> 6; matrix products, arithmetic and copies ran while one was open for 13% -> 7% of each run, Pallas kernels for 35% -> 35%
where the time goes in v1:
time: 183 us; the launch traced here: 182 us
  Pallas kernels  68.6 us (37%)
  waiting for transfers between devices  57.9 us (32%)
  starting transfers between devices  41 us (22%)
  matrix products  7.15 us (4%)
  local copies, waits for them, and re-layouts  4.4 us (2%)
  other arithmetic  3.07 us (2%)
    all_to_all x4, waiting for transfers between devices, exchange(): return lax.all_to_all(x, 'expert', split_axis=0, concat_axis=0, tiled=True)  50.9 us
    all_to_all x4, starting transfers between devices, exchange(): return lax.all_to_all(x, 'expert', split_axis=0, concat_axis=0, tiled=True)  39.2 us
    pallas_call x2, Pallas kernels, forward_call(): pl.pallas_call(functools.partial(forward_kernel, span, steps, cap), grid_...  31.8 us
    pallas_call x2, Pallas kernels, backward_call(): pl.pallas_call(functools.partial(backward_kernel, span, steps, cap), grid...  25.7 us
    ppermute x8, waiting for transfers between devices, swap(): return lax.ppermute(x, 'head', SWAP)  6.93 us
    dot_general x1, matrix products, per_device(): head_map = jnp.dot(w_down, head_weight, preferred_element_type=F32)  5.09 us
    pallas_call x1, Pallas kernels, per_device(): pl.pallas_call(functools.partial(last_combine_kernel, cap), out_shape=jax...  4.28 us
    pallas_call x1, Pallas kernels, first_rows(): pl.pallas_call(first_rows_kernel, grid_spec=pltpu.PrefetchScalarGridSpec(...  3.84 us
  transfers between devices with their start and end apart: 12, of which 6 were waited for; matrix products, arithmetic and copies ran while one was open for 7% of the time, Pallas kernels for 35%

profile of v1, /device:TPU:0, one launch (start us, length us, event | category | flops | bytes accessed | tf_op | source)
XLA Modules:
  0.0 182.5 jit_solution(15368166254272579210)
XLA Ops:
  0.0 0.5 collective-permute-start.1
  0.5 3.8 %shard_map.100 = (bf16[512,2304]{1,0:T(8,128)(2,1)}, f32[64,128]{1,0:T(8,128)}) custom-call(s32[1]{0:T(128)} %bitcast.head_ref, s32[8,128]{1,0:T(8,128)} %bitcast.87, bf16[128,4096]{1,0:T(8,128)(2,1)} %tok_ref.1), custom_call_target="tpu_custom_call" | custom-call | tf_op jit(solution)/shard_map/pallas_call | solution.py:442
  4.4 11.9 %all-to-all-start.1 = ((bf16[64,8,2304]{2,1,0:T(8,128)(2,1)}), bf16[64,8,2304]{2,1,0:T(8,128)(2,1)}, u32[]{:S(2)}, u32[]{:S(2)}) async-start(bf16[64,8,2304]{2,1,0:T(8,128)(2,1)} %bitcast.84), calls=%async_computation.1 | async-start | bytes 4718592 | tf_op jit(solution)/shard_map/all_to_all | solution.py:26
  16.4 0.1 copy.54
  16.5 0.2 reduce-window.4
  16.7 0.1 eq.77
  16.8 0.5 select_reduce_fusion
  17.4 0.4 convolution_bitcast_fusion
  17.7 0.2 select_reduce_fusion.1
  18.0 0.5 fusion.8
  18.5 0.1 copy.44
  18.7 0.3 copy.53
  18.9 0.2 copy.41
  19.3 0.7 select_n.49.refs_2_.refs_9_
  20.0 0.7 fusion.3
  20.7 0.1 multiply_bitcast_fusion
  20.9 0.4 fusion.5
  21.3 1.6 fusion.4.refs_0_
  23.0 5.1 %fusion.refs_1_.hm_ref.before_ref.after_ref = f32[1,768]{1,0:T(1,128)} fusion(bf16[4096,1]{0,1:T(2,128)(2,1)S(1)} %reshape.216, bf16[1,768,4096]{2,1,0:T(8,128)(2,1)} %param.14), kind=kOutput, calls=%fused_computation | convolution fusion | flops 6291456 | bytes 6302720 | tf_op jit(solution)/shard_map/dot_general | solution.py:658
  28.1 20.7 %all-to-all-done.1.refs_0_ = bf16[64,8,2304]{2,1,0:T(8,128)(2,1)} async-done(((bf16[64,8,2304]{2,1,0:T(8,128)(2,1)}), bf16[64,8,2304]{2,1,0:T(8,128)(2,1)}, u32[]{:S(2)}, u32[]{:S(2)}) %all-to-all-start.1) | async-done | bytes 2359328 | tf_op jit(solution)/shard_map/all_to_all | solution.py:26
  48.7 0.1 collective-permute-start.2
  48.8 6.4 %all-to-all-start = ((bf16[64,8,2432]{2,1,0:T(8,128)(2,1)}), bf16[64,8,2432]{2,1,0:T(8,128)(2,1)}, u32[]{:S(2)}, u32[]{:S(2)}) async-start(bf16[64,8,2432]{2,1,0:T(8,128)(2,1)} %shard_map.101.refs_1_), calls=%async_computation | async-start | bytes 4980736 | tf_op jit(solution)/shard_map/all_to_all | solution.py:26
  55.2 16.1 %shard_map.103 = (bf16[576,768]{1,0:T(8,128)(2,1)}, bf16[576,768]{1,0:T(8,128)(2,1)}, f32[64,128]{1,0:T(8,128)}) custom-call(s32[1]{0:T(128)} %bitcast.head_ref, bf16[512,2304]{1,0:T(8,128)(2,1)} %bitcast.23.own_hbm, bf16[512,2304]{1,0:T(8,128)(2,1)} %bitcast.24.other_hbm, bf16[4096,768]{1,0:T(8,128)(2,1)} %bitcast.74, bf16[4096,768]{1,0:T(8,128)(2,1)} %bitcast.79, ...), custom_call_target="tpu_custom_call" | custom-call | tf_op jit(solution)/shard_map/pallas_call | solution.py:221
  71.3 0.3 collective-permute-start.3
  71.6 0.3 collective-permute-start.4
  71.9 2.1 %collective-permute-done.3.refs_2_ = bf16[576,768]{1,0:T(8,128)(2,1)S(1)} collective-permute-done((bf16[576,768]{1,0:T(8,128)(2,1)}, bf16[576,768]{1,0:T(8,128)(2,1)S(1)}, u32[]{:S(2)}, u32[]{:S(2)}) %collective-permute-start.3) | collective-permute-done | bytes 884768 | tf_op jit(solution)/shard_map/ppermute | solution.py:30
  74.0 1.3 collective-permute-done.4.refs_3_
  75.3 0.9 copy-done.6
  76.2 12.5 %shard_map.104.refs_1_.after_ref = bf16[512,2304]{1,0:T(8,128)(2,1)} custom-call(s32[1]{0:T(128)} %bitcast.head_ref, bf16[576,768]{1,0:T(8,128)(2,1)} %get-tuple-element.15.refs_0_, bf16[576,768]{1,0:T(8,128)(2,1)} %get-tuple-element.16.refs_1_, bf16[576,768]{1,0:T(8,128)(2,1)} %copy-done.5, bf16[576,768]{1,0:T(8,128)(2,1)} %copy-done.6, ...), custom_call_target="tpu_custom_call" | custom-call | tf_op jit(solution)/shard_map/pallas_call | solution.py:371
  88.8 0.4 all-to-all-done.refs_0_
  89.2 10.4 %all-to-all-start.2 = ((bf16[64,8,2304]{2,1,0:T(8,128)(2,1)}), bf16[64,8,2304]{2,1,0:T(8,128)(2,1)}, u32[]{:S(2)}, u32[]{:S(2)}) async-start(bf16[64,8,2304]{2,1,0:T(8,128)(2,1)} %bitcast.27), calls=%async_computation.2 | async-start | bytes 4718592 | tf_op jit(solution)/shard_map/all_to_all | solution.py:26
  99.6 15.8 %shard_map.106 = (bf16[576,768]{1,0:T(8,128)(2,1)}, bf16[640,768]{1,0:T(8,128)(2,1)}, f32[64,128]{1,0:T(8,128)}) custom-call(s32[1]{0:T(128)} %bitcast.head_ref, bf16[512,2432]{1,0:T(8,128)(2,1)} %bitcast.25.own_hbm.refs_10_, bf16[512,2432]{1,0:T(8,128)(2,1)} %bitcast.26.other_hbm, bf16[4096,768]{1,0:T(8,128)(2,1)} %bitcast.76, bf16[4096,768]{1,0:T(8,128)(2,1)} %bitcast.81, ...), custom_call_target="tpu_custom_call" | custom-call | tf_op jit(solution)/shard_map/pallas_call | solution.py:221
  115.4 0.2 collective-permute-start.7
  115.5 0.4 collective-permute-start.6
  116.0 3.5 %collective-permute-done.6.refs_2_ = bf16[576,768]{1,0:T(8,128)(2,1)S(1)} collective-permute-done((bf16[576,768]{1,0:T(8,128)(2,1)}, bf16[576,768]{1,0:T(8,128)(2,1)S(1)}, u32[]{:S(2)}, u32[]{:S(2)}) %collective-permute-start.6) | collective-permute-done | bytes 884768 | tf_op jit(solution)/shard_map/ppermute | solution.py:30
  119.5 1.0 copy-done.4
  120.5 0.3 copy-done.3
  120.8 13.2 %shard_map.107.refs_0_ = bf16[512,2432]{1,0:T(8,128)(2,1)} custom-call(s32[1]{0:T(128)} %bitcast.head_ref, bf16[576,768]{1,0:T(8,128)(2,1)} %get-tuple-element.18.refs_0_, bf16[640,768]{1,0:T(8,128)(2,1)} %get-tuple-element.19.refs_1_, bf16[576,768]{1,0:T(8,128)(2,1)} %copy-done.4, bf16[640,768]{1,0:T(8,128)(2,1)} %copy-done.3, bf16[4096,768]{1,0:T(8,128)(2,1)} %bitcast.77, ...), custom_call_target="tpu_custom_call" | custom-call | tf_op jit(solution)/shard_map/pallas_call | solution.py:371
  134.0 10.6 %all-to-all-start.3 = ((bf16[64,8,2432]{2,1,0:T(8,128)(2,1)}), bf16[64,8,2432]{2,1,0:T(8,128)(2,1)}, u32[]{:S(2)}, u32[]{:S(2)}) async-start(bf16[64,8,2432]{2,1,0:T(8,128)(2,1)} %bitcast.83), calls=%async_computation.3 | async-start | bytes 4980736 | tf_op jit(solution)/shard_map/all_to_all | solution.py:26
  144.6 0.1 copy.49.prob_ref
  144.7 0.1 copy.48.slot_ref
  144.8 0.1 copy.50.pairs_ref
  145.0 0.1 copy.47
  145.1 0.1 reshape.214.lens_ref
  145.3 0.1 multiply_reduce_fusion.member_ref
  145.4 2.9 %shard_map.109.acc_ref = f32[128,2048]{1,0:T(8,128)S(1)} custom-call(bf16[512,2304]{1,0:T(8,128)(2,1)} %bitcast.30.home_ref, f32[128,64]{1,0:T(8,128)S(1)} %copy.48.slot_ref, f32[128,64]{1,0:T(8,128)S(1)} %copy.49.prob_ref, f32[1,2048]{1,0:T(1,128)S(1)} %bitcast.72), custom_call_target="tpu_custom_call" | custom-call | tf_op jit(solution)/shard_map/pallas_call | solution.py:698
  148.3 29.9 %all-to-all-done.3 = bf16[64,8,2432]{2,1,0:T(8,128)(2,1)} async-done(((bf16[64,8,2432]{2,1,0:T(8,128)(2,1)}), bf16[64,8,2432]{2,1,0:T(8,128)(2,1)}, u32[]{:S(2)}, u32[]{:S(2)}) %all-to-all-start.3) | async-done | bytes 2490400 | tf_op jit(solution)/shard_map/all_to_all | solution.py:26
  178.2 4.3 %shard_map.110 = bf16[128,2048]{1,0:T(8,128)(2,1)} custom-call(bf16[512,2432]{1,0:T(8,128)(2,1)} %bitcast.29.home_ref, f32[128,64]{1,0:T(8,128)S(1)} %copy.48.slot_ref, f32[128,64]{1,0:T(8,128)S(1)} %copy.49.prob_ref, f32[64,128]{1,0:T(8,128)S(1)} %copy-done.1, f32[64,128]{1,0:T(8,128)S(1)} %get-tuple-element.27.prob_et_ref, ...), custom_call_target="tpu_custom_call" | custom-call | tf_op jit(solution)/shard_map/pallas_call | solution.py:708
  (52 shorter events, 0.6 us)
Async XLA Ops:
  0.0 16.8 %copy-start = (bf16[4096,64]{0,1:T(8,128)(2,1)S(1)}, bf16[4096,64]{0,1:T(8,128)(2,1)}, u32[]{:S(2)}) copy-start(bf16[4096,64]{0,1:T(8,128)(2,1)} %param.11) | copy-start | bytes 1572868
  0.0 48.7 %collective-permute-start = (bf16[4096,768]{1,0:T(8,128)(2,1)}, bf16[4096,768]{1,0:T(8,128)(2,1)}, u32[]{:S(2)}, u32[]{:S(2)}) collective-permute-start(bf16[4096,768]{1,0:T(8,128)(2,1)} %bitcast.73), channel_id=1, source_target_pairs={{0,1},{1,0},{2,3},{3,2},{4,5},{5,4},{6,7},{7,6},{8,9},{9,8},{10,11... | collective-permute-start | bytes 18874376 | tf_op jit(solution)/shard_map/ppermute | solution.py:30
  0.0 48.7 %collective-permute-start.1 = (bf16[4096,768]{1,0:T(8,128)(2,1)}, bf16[4096,768]{1,0:T(8,128)(2,1)}, u32[]{:S(2)}, u32[]{:S(2)}) collective-permute-start(bf16[4096,768]{1,0:T(8,128)(2,1)} %bitcast.78), channel_id=1, source_target_pairs={{0,1},{1,0},{2,3},{3,2},{4,5},{5,4},{6,7},{7,6},{8,9},{9,8},{10,11... | collective-permute-start | bytes 18874376 | tf_op jit(solution)/shard_map/ppermute | solution.py:30
  4.4 12.0 %copy-start.8 = (s32[64,4]{0,1:T(4,128)S(1)}, s32[64,4]{0,1:T(4,128)}, u32[]{:S(2)}) copy-start(s32[64,4]{0,1:T(4,128)} %param.17) | copy-start | bytes 3076
  4.4 12.3 %copy-start.7 = (bf16[4096]{0:T(1024)(128)(2,1)S(1)}, bf16[4096]{0:T(1024)(128)(2,1)}, u32[]{:S(2)}) copy-start(bf16[4096]{0:T(1024)(128)(2,1)} %param.15) | copy-start | bytes 24580
  4.4 12.4 %copy-start.1 = (f32[64,128]{1,0:T(8,128)S(1)}, f32[64,128]{1,0:T(8,128)}, u32[]{:S(2)}) copy-start(f32[64,128]{1,0:T(8,128)} %get-tuple-element.13.slot_et_ref) | copy-start | bytes 98308
  4.4 12.4 %copy-start.2 = (bf16[128,4096]{1,0:T(8,128)(2,1)S(1)}, bf16[128,4096]{1,0:T(8,128)(2,1)}, u32[]{:S(2)}) copy-start(bf16[128,4096]{1,0:T(8,128)(2,1)} %tok_ref.1) | copy-start | bytes 3145732
  4.4 44.3 %all-to-all-start.1 = ((bf16[64,8,2304]{2,1,0:T(8,128)(2,1)}), bf16[64,8,2304]{2,1,0:T(8,128)(2,1)}, u32[]{:S(2)}, u32[]{:S(2)}) async-start(bf16[64,8,2304]{2,1,0:T(8,128)(2,1)} %bitcast.84), calls=%async_computation.1 | async-start | bytes 4718592 | tf_op jit(solution)/shard_map/all_to_all | solution.py:26
  16.3 1.7 copy-start.10
  48.7 6.5 %collective-permute-start.2 = (bf16[64,8,2304]{2,1,0:T(8,128)(2,1)}, bf16[64,8,2304]{2,1,0:T(8,128)(2,1)}, u32[]{:S(2)}, u32[]{:S(2)}) collective-permute-start(bf16[64,8,2304]{2,1,0:T(8,128)(2,1)} %shard_map.102), channel_id=1, source_target_pairs={{0,1},{1,0},{2,3},{3,2},{4,5},{5,4},{6,7},{7,6},{8,9},{9,8},{10,11... | collective-permute-start | bytes 7077896 | tf_op jit(solution)/shard_map/ppermute | solution.py:30
  48.8 40.3 %all-to-all-start = ((bf16[64,8,2432]{2,1,0:T(8,128)(2,1)}), bf16[64,8,2432]{2,1,0:T(8,128)(2,1)}, u32[]{:S(2)}, u32[]{:S(2)}) async-start(bf16[64,8,2432]{2,1,0:T(8,128)(2,1)} %shard_map.101.refs_1_), calls=%async_computation | async-start | bytes 4980736 | tf_op jit(solution)/shard_map/all_to_all | solution.py:26
  71.3 2.7 %collective-permute-start.3 = (bf16[576,768]{1,0:T(8,128)(2,1)}, bf16[576,768]{1,0:T(8,128)(2,1)S(1)}, u32[]{:S(2)}, u32[]{:S(2)}) collective-permute-start(bf16[576,768]{1,0:T(8,128)(2,1)} %get-tuple-element.15.refs_0_), channel_id=1, source_target_pairs={{0,1},{1,0},{2,3},{3,2},{4,5},{5,4},{6,7},{7,6},{8,9},{9,8},{10,11... | collective-permute-start | bytes 2654216 | tf_op jit(solution)/shard_map/ppermute | solution.py:30
  71.6 3.7 %collective-permute-start.4 = (bf16[576,768]{1,0:T(8,128)(2,1)}, bf16[576,768]{1,0:T(8,128)(2,1)S(1)}, u32[]{:S(2)}, u32[]{:S(2)}) collective-permute-start(bf16[576,768]{1,0:T(8,128)(2,1)} %get-tuple-element.16.refs_1_), channel_id=1, source_target_pairs={{0,1},{1,0},{2,3},{3,2},{4,5},{5,4},{6,7},{7,6},{8,9},{9,8},{10,11... | collective-permute-start | bytes 2654216 | tf_op jit(solution)/shard_map/ppermute | solution.py:30
  74.0 1.3 copy-start.5
  75.3 0.9 copy-start.6
  89.2 10.4 %collective-permute-start.5 = (bf16[64,8,2432]{2,1,0:T(8,128)(2,1)}, bf16[64,8,2432]{2,1,0:T(8,128)(2,1)}, u32[]{:S(2)}, u32[]{:S(2)}) collective-permute-start(bf16[64,8,2432]{2,1,0:T(8,128)(2,1)} %shard_map.105), channel_id=1, source_target_pairs={{0,1},{1,0},{2,3},{3,2},{4,5},{5,4},{6,7},{7,6},{8,9},{9,8},{10,11... | collective-permute-start | bytes 7471112 | tf_op jit(solution)/shard_map/ppermute | solution.py:30
  89.2 44.9 %all-to-all-start.2 = ((bf16[64,8,2304]{2,1,0:T(8,128)(2,1)}), bf16[64,8,2304]{2,1,0:T(8,128)(2,1)}, u32[]{:S(2)}, u32[]{:S(2)}) async-start(bf16[64,8,2304]{2,1,0:T(8,128)(2,1)} %bitcast.27), calls=%async_computation.2 | async-start | bytes 4718592 | tf_op jit(solution)/shard_map/all_to_all | solution.py:26
  115.4 4.1 %collective-permute-start.7 = (bf16[640,768]{1,0:T(8,128)(2,1)}, bf16[640,768]{1,0:T(8,128)(2,1)S(1)}, u32[]{:S(2)}, u32[]{:S(2)}) collective-permute-start(bf16[640,768]{1,0:T(8,128)(2,1)} %get-tuple-element.19.refs_1_), channel_id=1, source_target_pairs={{0,1},{1,0},{2,3},{3,2},{4,5},{5,4},{6,7},{7,6},{8,9},{9,8},{10,11... | collective-permute-start | bytes 2949128 | tf_op jit(solution)/shard_map/ppermute | solution.py:30
  115.5 4.0 %collective-permute-start.6 = (bf16[576,768]{1,0:T(8,128)(2,1)}, bf16[576,768]{1,0:T(8,128)(2,1)S(1)}, u32[]{:S(2)}, u32[]{:S(2)}) collective-permute-start(bf16[576,768]{1,0:T(8,128)(2,1)} %get-tuple-element.18.refs_0_), channel_id=1, source_target_pairs={{0,1},{1,0},{2,3},{3,2},{4,5},{5,4},{6,7},{7,6},{8,9},{9,8},{10,11... | collective-permute-start | bytes 2654216 | tf_op jit(solution)/shard_map/ppermute | solution.py:30
  119.5 1.0 copy-start.4
  119.5 1.3 copy-start.3
  134.0 10.8 %copy-start.9 = (s32[128,2]{0,1:T(2,128)S(1)}, s32[128,2]{0,1:T(2,128)}, u32[]{:S(2)}) copy-start(s32[128,2]{0,1:T(2,128)} %param.18) | copy-start | bytes 3076
  134.0 44.2 %all-to-all-start.3 = ((bf16[64,8,2432]{2,1,0:T(8,128)(2,1)}), bf16[64,8,2432]{2,1,0:T(8,128)(2,1)}, u32[]{:S(2)}, u32[]{:S(2)}) async-start(bf16[64,8,2432]{2,1,0:T(8,128)(2,1)} %bitcast.83), calls=%async_computation.3 | async-start | bytes 4980736 | tf_op jit(solution)/shard_map/all_to_all | solution.py:26

commit v2 on v1

--- a/solution.py
+++ b/solution.py
@@ -680,6 +680,7 @@
     recv_b = touch(recv_b, total_a)
     home_a = exchange(total_a.reshape(groups, MAIN, -1))
     dg_b, du_b, score_b = forward(cap, recv_b, score_a, total_a)
+    score_b = touch(score_b, limit=127 << 19)
     grads_b = (dg_b, du_b, swap(dg_b), swap(du_b))
     total_b = backward_call(
         cap,

time: 183 us -> 186 us (1.016)
  local copies, waits for them, and re-layouts: 4.4 us -> 13.2 us
  waiting for transfers between devices: 57.9 us -> 52.7 us
  Pallas kernels: 68.6 us -> 66.7 us
    unnamed x27 -> x43, local copies, waits for them, and re-layouts: 2.8 us -> 9.7 us
    all_to_all x4, waiting for transfers between devices: 50.9 us -> 45.7 us  [exchange(): return lax.all_to_all(x, 'expert', split_axis=0, concat_axis=0, tiled=True)]
  transfers between devices with their start and end apart: 12 -> 12, of which waited for: 6 -> 6; matrix products, arithmetic and copies ran while one was open for 7% -> 9% of each run, Pallas kernels for 35% -> 35%
where the time goes in v2:
time: 186 us; the launch traced here: 185 us
  Pallas kernels  66.7 us (36%)
  waiting for transfers between devices  52.7 us (28%)
  starting transfers between devices  40.7 us (22%)
  local copies, waits for them, and re-layouts  13.2 us (7%)
  matrix products  7.16 us (4%)
  other arithmetic  4.32 us (2%)
    all_to_all x4, waiting for transfers between devices, exchange(): return lax.all_to_all(x, 'expert', split_axis=0, concat_axis=0, tiled=True)  45.7 us
    all_to_all x4, starting transfers between devices, exchange(): return lax.all_to_all(x, 'expert', split_axis=0, concat_axis=0, tiled=True)  38.9 us
    pallas_call x2, Pallas kernels, forward_call(): pl.pallas_call(functools.partial(forward_kernel, span, steps, cap), grid_...  31.7 us
    pallas_call x2, Pallas kernels, backward_call(): pl.pallas_call(functools.partial(backward_kernel, span, steps, cap), grid...  25.8 us
    unnamed x43, local copies, waits for them, and re-layouts  9.7 us
    ppermute x8, waiting for transfers between devices, swap(): return lax.ppermute(x, 'head', SWAP)  7.06 us
    dot_general x1, matrix products, per_device(): head_map = jnp.dot(w_down, head_weight, preferred_element_type=F32)  5.11 us
    pallas_call x1, Pallas kernels, first_rows(): pl.pallas_call(first_rows_kernel, grid_spec=pltpu.PrefetchScalarGridSpec(...  3.81 us
  transfers between devices with their start and end apart: 12, of which 6 were waited for; matrix products, arithmetic and copies ran while one was open for 9% of the time, Pallas kernels for 35%

profile of v2, /device:TPU:0, one launch (start us, length us, event | category | flops | bytes accessed | tf_op | source)
XLA Modules:
  0.0 185.3 jit_solution(10292283051237509878)
XLA Ops:
  0.0 0.5 collective-permute-start.1
  0.5 3.8 %shard_map.100 = (bf16[512,2304]{1,0:T(8,128)(2,1)}, f32[64,128]{1,0:T(8,128)}) custom-call(s32[1]{0:T(128)} %bitcast.head_ref, s32[8,128]{1,0:T(8,128)} %bitcast.88, bf16[128,4096]{1,0:T(8,128)(2,1)} %tok_ref.1), custom_call_target="tpu_custom_call" | custom-call | tf_op jit(solution)/shard_map/pallas_call | solution.py:442
  4.4 11.9 %all-to-all-start.1 = ((bf16[64,8,2304]{2,1,0:T(8,128)(2,1)}), bf16[64,8,2304]{2,1,0:T(8,128)(2,1)}, u32[]{:S(2)}, u32[]{:S(2)}) async-start(bf16[64,8,2304]{2,1,0:T(8,128)(2,1)} %bitcast.85), calls=%async_computation.1 | async-start | bytes 4718592 | tf_op jit(solution)/shard_map/all_to_all | solution.py:26
  16.8 0.5 select_reduce_fusion
  17.3 0.4 convolution_bitcast_fusion
  17.7 0.2 select_reduce_fusion.1
  17.9 0.6 broadcast_multiply_fusion
  18.6 0.5 fusion.8
  19.2 0.3 copy.54
  19.5 0.2 copy.42
  19.8 0.7 select_n.49.refs_2_.refs_9_
  20.5 0.7 fusion.3
  21.4 0.4 fusion.5
  21.9 1.6 fusion.4.refs_0_
  23.5 5.1 %fusion.refs_1_.hm_ref.before_ref.after_ref = f32[1,768]{1,0:T(1,128)} fusion(bf16[4096,1]{0,1:T(2,128)(2,1)S(1)} %reshape.216, bf16[1,768,4096]{2,1,0:T(8,128)(2,1)} %param.14), kind=kOutput, calls=%fused_computation | convolution fusion | flops 6291456 | bytes 6302720 | tf_op jit(solution)/shard_map/dot_general | solution.py:658
  28.6 20.0 %all-to-all-done.1.refs_0_ = bf16[64,8,2304]{2,1,0:T(8,128)(2,1)} async-done(((bf16[64,8,2304]{2,1,0:T(8,128)(2,1)}), bf16[64,8,2304]{2,1,0:T(8,128)(2,1)}, u32[]{:S(2)}, u32[]{:S(2)}) %all-to-all-start.1) | async-done | bytes 2359328 | tf_op jit(solution)/shard_map/all_to_all | solution.py:26
  48.7 6.3 %all-to-all-start = ((bf16[64,8,2432]{2,1,0:T(8,128)(2,1)}), bf16[64,8,2432]{2,1,0:T(8,128)(2,1)}, u32[]{:S(2)}, u32[]{:S(2)}) async-start(bf16[64,8,2432]{2,1,0:T(8,128)(2,1)} %shard_map.101.refs_1_), calls=%async_computation | async-start | bytes 4980736 | tf_op jit(solution)/shard_map/all_to_all | solution.py:26
  55.1 16.0 %shard_map.103 = (bf16[576,768]{1,0:T(8,128)(2,1)}, bf16[576,768]{1,0:T(8,128)(2,1)}, f32[64,128]{1,0:T(8,128)}) custom-call(s32[1]{0:T(128)} %bitcast.head_ref, bf16[512,2304]{1,0:T(8,128)(2,1)} %bitcast.23.own_hbm, bf16[512,2304]{1,0:T(8,128)(2,1)} %bitcast.24.other_hbm, bf16[4096,768]{1,0:T(8,128)(2,1)} %bitcast.75, bf16[4096,768]{1,0:T(8,128)(2,1)} %bitcast.80, ...), custom_call_target="tpu_custom_call" | custom-call | tf_op jit(solution)/shard_map/pallas_call | solution.py:221
  71.0 0.4 collective-permute-start.3
  71.4 0.2 collective-permute-start.4
  71.6 2.1 %collective-permute-done.3.refs_2_ = bf16[576,768]{1,0:T(8,128)(2,1)S(1)} collective-permute-done((bf16[576,768]{1,0:T(8,128)(2,1)}, bf16[576,768]{1,0:T(8,128)(2,1)S(1)}, u32[]{:S(2)}, u32[]{:S(2)}) %collective-permute-start.3) | collective-permute-done | bytes 884768 | tf_op jit(solution)/shard_map/ppermute | solution.py:30
  73.7 1.3 collective-permute-done.4.refs_3_
  75.0 0.9 copy-done.14
  75.9 12.5 %shard_map.104.refs_1_.after_ref = bf16[512,2304]{1,0:T(8,128)(2,1)} custom-call(s32[1]{0:T(128)} %bitcast.head_ref, bf16[576,768]{1,0:T(8,128)(2,1)} %get-tuple-element.15.refs_0_, bf16[576,768]{1,0:T(8,128)(2,1)} %get-tuple-element.16.refs_1_, bf16[576,768]{1,0:T(8,128)(2,1)} %copy-done.13, bf16[576,768]{1,0:T(8,128)(2,1)} %copy-done.14, ...), custom_call_target="tpu_custom_call" | custom-call | tf_op jit(solution)/shard_map/pallas_call | solution.py:371
  88.5 0.5 all-to-all-done.refs_0_
  89.0 10.3 %all-to-all-start.2 = ((bf16[64,8,2304]{2,1,0:T(8,128)(2,1)}), bf16[64,8,2304]{2,1,0:T(8,128)(2,1)}, u32[]{:S(2)}, u32[]{:S(2)}) async-start(bf16[64,8,2304]{2,1,0:T(8,128)(2,1)} %bitcast.27), calls=%async_computation.2 | async-start | bytes 4718592 | tf_op jit(solution)/shard_map/all_to_all | solution.py:26
  99.3 15.8 %shard_map.106 = (bf16[576,768]{1,0:T(8,128)(2,1)}, bf16[640,768]{1,0:T(8,128)(2,1)}, f32[64,128]{1,0:T(8,128)}) custom-call(s32[1]{0:T(128)} %bitcast.head_ref, bf16[512,2432]{1,0:T(8,128)(2,1)} %bitcast.25.own_hbm.refs_10_, bf16[512,2432]{1,0:T(8,128)(2,1)} %bitcast.26.other_hbm, bf16[4096,768]{1,0:T(8,128)(2,1)} %bitcast.77, bf16[4096,768]{1,0:T(8,128)(2,1)} %bitcast.82, ...), custom_call_target="tpu_custom_call" | custom-call | tf_op jit(solution)/shard_map/pallas_call | solution.py:221
  115.2 0.4 collective-permute-start.6
  115.6 3.7 %collective-permute-done.6.refs_2_ = bf16[576,768]{1,0:T(8,128)(2,1)} collective-permute-done((bf16[576,768]{1,0:T(8,128)(2,1)}, bf16[576,768]{1,0:T(8,128)(2,1)}, u32[]{:S(2)}, u32[]{:S(2)}) %collective-permute-start.6) | collective-permute-done | bytes 884768 | tf_op jit(solution)/shard_map/ppermute | solution.py:30
  119.3 13.2 %shard_map.108.refs_0_ = bf16[512,2432]{1,0:T(8,128)(2,1)} custom-call(s32[1]{0:T(128)} %bitcast.head_ref, bf16[576,768]{1,0:T(8,128)(2,1)} %get-tuple-element.18.refs_0_, bf16[640,768]{1,0:T(8,128)(2,1)} %get-tuple-element.19.refs_1_, bf16[576,768]{1,0:T(8,128)(2,1)} %collective-permute-done.6.refs_2_, bf16[640,768]{1,0:T(8,128)(2,1)} %collective-permute-done.7.refs_3_, ...), custom_call_target="tpu_custom_call" | custom-call | tf_op jit(solution)/shard_map/pallas_call | solution.py:371
  132.6 10.5 %all-to-all-start.3 = ((bf16[64,8,2432]{2,1,0:T(8,128)(2,1)}), bf16[64,8,2432]{2,1,0:T(8,128)(2,1)S(1)}, u32[]{:S(2)}, u32[]{:S(2)}) async-start(bf16[64,8,2432]{2,1,0:T(8,128)(2,1)} %bitcast.84), calls=%async_computation.3 | async-start | bytes 4980736 | tf_op jit(solution)/shard_map/all_to_all | solution.py:26
  143.1 0.7 copy.50.prob_ref
  143.8 0.7 copy.49.slot_ref
  144.6 0.7 copy.51.pairs_ref
  145.6 0.8 multiply_reduce_fusion.member_ref
  146.4 0.7 dynamic-slice_bitcast_fusion.router_ref
  147.1 0.8 copy-done.3
  148.0 0.8 copy-done.5
  148.8 2.9 %shard_map.110.acc_ref = f32[128,2048]{1,0:T(8,128)S(1)} custom-call(bf16[512,2304]{1,0:T(8,128)(2,1)} %bitcast.30.home_ref, f32[128,64]{1,0:T(8,128)S(1)} %copy-done.5, f32[128,64]{1,0:T(8,128)S(1)} %copy-done.3, f32[1,2048]{1,0:T(1,128)S(1)} %bitcast.73), custom_call_target="tpu_custom_call" | custom-call | tf_op jit(solution)/shard_map/pallas_call | solution.py:699
  151.7 25.1 %all-to-all-done.3 = bf16[64,8,2432]{2,1,0:T(8,128)(2,1)S(1)} async-done(((bf16[64,8,2432]{2,1,0:T(8,128)(2,1)}), bf16[64,8,2432]{2,1,0:T(8,128)(2,1)S(1)}, u32[]{:S(2)}, u32[]{:S(2)}) %all-to-all-start.3) | async-done | bytes 2490400 | tf_op jit(solution)/shard_map/all_to_all | solution.py:26
  176.8 0.9 copy-done
  177.8 0.8 copy-done.2
  178.5 0.8 copy-done.4
  179.4 0.8 copy-done.6
  180.2 0.9 copy-done.7
  181.1 0.8 copy-done.8
  181.9 0.8 copy-done.9
  182.7 2.6 %shard_map.111 = bf16[128,2048]{1,0:T(8,128)(2,1)} custom-call(bf16[512,2432]{1,0:T(8,128)(2,1)S(1)} %bitcast.71, f32[128,64]{1,0:T(8,128)S(1)} %copy-done.6, f32[128,64]{1,0:T(8,128)S(1)} %copy-done.4, f32[64,128]{1,0:T(8,128)S(1)} %copy-done.2, f32[64,128]{1,0:T(8,128)S(1)} %copy-done.9, f32[128,2048]{1,0:T(8,128)S(1)} %shard_map.110.acc_ref, ...), custom_call_target="tpu_custom_call" | custom-call | tf_op jit(solution)/shard_map/pallas_call | solution.py:709
  (69 shorter events, 1.6 us)
Async XLA Ops:
  0.0 48.6 %collective-permute-start = (bf16[4096,768]{1,0:T(8,128)(2,1)}, bf16[4096,768]{1,0:T(8,128)(2,1)}, u32[]{:S(2)}, u32[]{:S(2)}) collective-permute-start(bf16[4096,768]{1,0:T(8,128)(2,1)} %bitcast.74), channel_id=1, source_target_pairs={{0,1},{1,0},{2,3},{3,2},{4,5},{5,4},{6,7},{7,6},{8,9},{9,8},{10,11... | collective-permute-start | bytes 18874376 | tf_op jit(solution)/shard_map/ppermute | solution.py:30
  0.0 48.6 %collective-permute-start.1 = (bf16[4096,768]{1,0:T(8,128)(2,1)}, bf16[4096,768]{1,0:T(8,128)(2,1)}, u32[]{:S(2)}, u32[]{:S(2)}) collective-permute-start(bf16[4096,768]{1,0:T(8,128)(2,1)} %bitcast.79), channel_id=1, source_target_pairs={{0,1},{1,0},{2,3},{3,2},{4,5},{5,4},{6,7},{7,6},{8,9},{9,8},{10,11... | collective-permute-start | bytes 18874376 | tf_op jit(solution)/shard_map/ppermute | solution.py:30
  4.3 12.0 %copy-start.16 = (s32[64,4]{0,1:T(4,128)S(1)}, s32[64,4]{0,1:T(4,128)}, u32[]{:S(2)}) copy-start(s32[64,4]{0,1:T(4,128)} %param.17) | copy-start | bytes 3076
  4.3 12.3 %copy-start.15 = (bf16[4096]{0:T(1024)(128)(2,1)S(1)}, bf16[4096]{0:T(1024)(128)(2,1)}, u32[]{:S(2)}) copy-start(bf16[4096]{0:T(1024)(128)(2,1)} %param.15) | copy-start | bytes 24580
  4.4 12.4 %copy-start.1 = (f32[64,128]{1,0:T(8,128)S(1)}, f32[64,128]{1,0:T(8,128)}, u32[]{:S(2)}) copy-start(f32[64,128]{1,0:T(8,128)} %get-tuple-element.13.slot_et_ref) | copy-start | bytes 98308
  4.4 12.4 %copy-start.10 = (bf16[128,4096]{1,0:T(8,128)(2,1)S(1)}, bf16[128,4096]{1,0:T(8,128)(2,1)}, u32[]{:S(2)}) copy-start(bf16[128,4096]{1,0:T(8,128)(2,1)} %tok_ref.1) | copy-start | bytes 3145732
  4.4 12.4 %copy-start.11 = (bf16[4096,64]{0,1:T(8,128)(2,1)S(1)}, bf16[4096,64]{0,1:T(8,128)(2,1)}, u32[]{:S(2)}) copy-start(bf16[4096,64]{0,1:T(8,128)(2,1)} %param.11) | copy-start | bytes 1572868
  4.4 44.2 %all-to-all-start.1 = ((bf16[64,8,2304]{2,1,0:T(8,128)(2,1)}), bf16[64,8,2304]{2,1,0:T(8,128)(2,1)}, u32[]{:S(2)}, u32[]{:S(2)}) async-start(bf16[64,8,2304]{2,1,0:T(8,128)(2,1)} %bitcast.85), calls=%async_computation.1 | async-start | bytes 4718592 | tf_op jit(solution)/shard_map/all_to_all | solution.py:26
  16.3 2.3 %copy-start.18 = (s32[18]{0:T(128)S(1)}, s32[18]{0:T(128)}, u32[]{:S(2)}) copy-start(s32[18]{0:T(128)} %constant.36.clone) | copy-start | bytes 220
  48.6 6.4 %collective-permute-start.2 = (bf16[64,8,2304]{2,1,0:T(8,128)(2,1)}, bf16[64,8,2304]{2,1,0:T(8,128)(2,1)}, u32[]{:S(2)}, u32[]{:S(2)}) collective-permute-start(bf16[64,8,2304]{2,1,0:T(8,128)(2,1)} %shard_map.102), channel_id=1, source_target_pairs={{0,1},{1,0},{2,3},{3,2},{4,5},{5,4},{6,7},{7,6},{8,9},{9,8},{10,11... | collective-permute-start | bytes 7077896 | tf_op jit(solution)/shard_map/ppermute | solution.py:30
  48.7 40.2 %all-to-all-start = ((bf16[64,8,2432]{2,1,0:T(8,128)(2,1)}), bf16[64,8,2432]{2,1,0:T(8,128)(2,1)}, u32[]{:S(2)}, u32[]{:S(2)}) async-start(bf16[64,8,2432]{2,1,0:T(8,128)(2,1)} %shard_map.101.refs_1_), calls=%async_computation | async-start | bytes 4980736 | tf_op jit(solution)/shard_map/all_to_all | solution.py:26
  71.0 2.7 %collective-permute-start.3 = (bf16[576,768]{1,0:T(8,128)(2,1)}, bf16[576,768]{1,0:T(8,128)(2,1)S(1)}, u32[]{:S(2)}, u32[]{:S(2)}) collective-permute-start(bf16[576,768]{1,0:T(8,128)(2,1)} %get-tuple-element.15.refs_0_), channel_id=1, source_target_pairs={{0,1},{1,0},{2,3},{3,2},{4,5},{5,4},{6,7},{7,6},{8,9},{9,8},{10,11... | collective-permute-start | bytes 2654216 | tf_op jit(solution)/shard_map/ppermute | solution.py:30
  71.4 3.6 %collective-permute-start.4 = (bf16[576,768]{1,0:T(8,128)(2,1)}, bf16[576,768]{1,0:T(8,128)(2,1)S(1)}, u32[]{:S(2)}, u32[]{:S(2)}) collective-permute-start(bf16[576,768]{1,0:T(8,128)(2,1)} %get-tuple-element.16.refs_1_), channel_id=1, source_target_pairs={{0,1},{1,0},{2,3},{3,2},{4,5},{5,4},{6,7},{7,6},{8,9},{9,8},{10,11... | collective-permute-start | bytes 2654216 | tf_op jit(solution)/shard_map/ppermute | solution.py:30
  73.7 1.3 copy-start.13
  75.0 0.9 copy-start.14
  89.0 10.3 %collective-permute-start.5 = (bf16[64,8,2432]{2,1,0:T(8,128)(2,1)}, bf16[64,8,2432]{2,1,0:T(8,128)(2,1)}, u32[]{:S(2)}, u32[]{:S(2)}) collective-permute-start(bf16[64,8,2432]{2,1,0:T(8,128)(2,1)} %shard_map.105), channel_id=1, source_target_pairs={{0,1},{1,0},{2,3},{3,2},{4,5},{5,4},{6,7},{7,6},{8,9},{9,8},{10,11... | collective-permute-start | bytes 7471112 | tf_op jit(solution)/shard_map/ppermute | solution.py:30
  89.0 43.6 %all-to-all-start.2 = ((bf16[64,8,2304]{2,1,0:T(8,128)(2,1)}), bf16[64,8,2304]{2,1,0:T(8,128)(2,1)}, u32[]{:S(2)}, u32[]{:S(2)}) async-start(bf16[64,8,2304]{2,1,0:T(8,128)(2,1)} %bitcast.27), calls=%async_computation.2 | async-start | bytes 4718592 | tf_op jit(solution)/shard_map/all_to_all | solution.py:26
  115.1 4.3 %collective-permute-start.7 = (bf16[640,768]{1,0:T(8,128)(2,1)}, bf16[640,768]{1,0:T(8,128)(2,1)}, u32[]{:S(2)}, u32[]{:S(2)}) collective-permute-start(bf16[640,768]{1,0:T(8,128)(2,1)} %get-tuple-element.19.refs_1_), channel_id=1, source_target_pairs={{0,1},{1,0},{2,3},{3,2},{4,5},{5,4},{6,7},{7,6},{8,9},{9,8},{10,11... | collective-permute-start | bytes 2949128 | tf_op jit(solution)/shard_map/ppermute | solution.py:30
  115.2 4.1 %collective-permute-start.6 = (bf16[576,768]{1,0:T(8,128)(2,1)}, bf16[576,768]{1,0:T(8,128)(2,1)}, u32[]{:S(2)}, u32[]{:S(2)}) collective-permute-start(bf16[576,768]{1,0:T(8,128)(2,1)} %get-tuple-element.18.refs_0_), channel_id=1, source_target_pairs={{0,1},{1,0},{2,3},{3,2},{4,5},{5,4},{6,7},{7,6},{8,9},{9,8},{10,11... | collective-permute-start | bytes 2654216 | tf_op jit(solution)/shard_map/ppermute | solution.py:30
  132.6 12.0 %copy-start.17 = (s32[128,2]{0,1:T(2,128)S(1)}, s32[128,2]{0,1:T(2,128)}, u32[]{:S(2)}) copy-start(s32[128,2]{0,1:T(2,128)} %param.18) | copy-start | bytes 3076
  132.6 13.8 %copy-start.12 = (bf16[4096,64]{0,1:T(8,128)(2,1)S(1)}, bf16[4096,64]{0,1:T(8,128)(2,1)}, u32[]{:S(2)}) copy-start(bf16[4096,64]{0,1:T(8,128)(2,1)} %param.11) | copy-start | bytes 1572868
  132.6 44.2 %all-to-all-start.3 = ((bf16[64,8,2432]{2,1,0:T(8,128)(2,1)}), bf16[64,8,2432]{2,1,0:T(8,128)(2,1)S(1)}, u32[]{:S(2)}, u32[]{:S(2)}) async-start(bf16[64,8,2432]{2,1,0:T(8,128)(2,1)} %bitcast.84), calls=%async_computation.3 | async-start | bytes 4980736 | tf_op jit(solution)/shard_map/all_to_all | solution.py:26
  147.1 0.8 copy-start.3
  148.0 0.8 copy-start.5
  176.8 1.0 copy-start
  177.8 0.8 copy-start.2
  178.5 0.8 copy-start.4
  179.4 0.8 copy-start.6
  180.2 0.9 copy-start.7
  181.1 0.8 copy-start.8
  181.9 0.8 copy-start.9
